TPU v7x, 256 devices: a whole 4x4x8 slice. The times are simulated.
256 devices in a mesh: filt: 8 (over z_hi, core), space: 32 (over y, x, z_lo).
Axes of the slice: x: 4, y: 4, z: 8 (z_hi: 4, z_lo: 2; z = z_hi * 2 + z_lo), core: 2. Of those that a mesh axis runs over, the one named last changes fastest.
Arguments:
- activation: bfloat16 [32, 64, 128, 256], P(None, 'space', 'filt'), may hold values from -6 to 6
- preact: bfloat16 [32, 64, 128, 256], P(None, 'space', 'filt'), may hold values from -6 to 6
- grad_out: bfloat16 [64, 32, 64, 128], P('filt', 'space'), may hold values from -6 to 6
- weight_a: bfloat16 [27, 32, 32], replicated, may hold values from -0.21875 to 0.21875
- weight_b: bfloat16 [27, 64, 32], P(None, 'filt'), may hold values from -0.625 to 0.625
Outputs:
- grad_input: bfloat16 [32, 64, 128, 256], P(None, 'space', 'filt')
- grad_wa: float32 [27, 32, 32], replicated
- grad_wb: float32 [27, 64, 32], P(None, 'filt')
All inputs are finite; a program needn't handle non-finite values.
Results may differ from a plain program's by a relative error of at most 0.0049.
Values may be sent and summed in bfloat16 or wider, within the bound.
A program may use at most 128 MiB of HBM per device.

v0:
```python
import math

import jax
import jax.numpy as jnp
from jax import lax
from jax.sharding import PartitionSpec as P


def with_halo(cells, sides, width):
    for axis, dim in sides:
        count = lax.axis_size(axis)
        ends = count - 1
        head = lax.slice_in_dim(cells, 0, width, axis=dim)
        tail = lax.slice_in_dim(cells, cells.shape[dim] - width, cells.shape[dim], axis=dim)
        cells = jnp.concatenate(
            [
                lax.ppermute(tail, axis, [(i, (i + 1) % count) for i in range(ends)]),
                cells,
                lax.ppermute(head, axis, [((i + 1) % count, i) for i in range(ends)]),
            ],
            axis=dim,
        )
    return cells


def tap_list():
    result = []
    for dx in (-1, 0, 1):
        for dy in (-1, 0, 1):
            for dz in (-1, 0, 1):
                result.append((1 - dx, 1 - dy, 1 - dz))
    return result


def input_grad(padded, weight, shape):
    total = jnp.zeros((weight.shape[2],) + shape, jnp.float32)
    for index, start in enumerate(tap_list()):
        piece = padded[
            :,
            start[0] : start[0] + shape[0],
            start[1] : start[1] + shape[1],
            start[2] : start[2] + shape[2],
        ]
        total = total + jnp.einsum(
            "oi,oxyz->ixyz", weight[index], piece, preferred_element_type=jnp.float32
        )
    return total


def weight_grad(padded, field):
    shape = field.shape[1:]
    terms = []
    for start in tap_list():
        piece = padded[
            :,
            start[0] : start[0] + shape[0],
            start[1] : start[1] + shape[1],
            start[2] : start[2] + shape[2],
        ]
        terms.append(jnp.einsum("oxyz,ixyz->oi", piece, field, preferred_element_type=jnp.float32))
    return jnp.stack(terms)


def per_device(activation, preact, grad_out, weight_a, weight_b):
    fine = preact.astype(jnp.float32)
    chans, sx, sy, sz = fine.shape
    blocks = jnp.maximum(fine, 0.0).reshape(chans, sx // 2, 2, sy // 2, 2, sz // 2, 2)
    pooled = jnp.mean(blocks, axis=(2, 4, 6)).astype(jnp.bfloat16)
    planes = grad_out.shape[1]
    full_rows = grad_out.shape[2]
    depth = grad_out.shape[3]
    space_count = lax.axis_size("space")
    coarse_cells = planes * space_count * full_rows * depth
    scale_b = 1.0 / math.sqrt(coarse_cells)
    scale_a = 1.0 / math.sqrt(8 * coarse_cells)
    rimmed = with_halo(grad_out, (("space", 1),), 1)
    padded = jnp.pad(rimmed, ((0, 0), (0, 0), (1, 1), (1, 1)))
    partial_grad = input_grad(padded, weight_b, (planes, full_rows, depth))
    grad_pooled = lax.psum_scatter(partial_grad, "filt", scatter_dimension=2, tiled=True).astype(
        jnp.bfloat16
    )
    all_pooled = lax.all_gather(pooled, "filt", axis=2, tiled=True)
    local_terms = weight_grad(padded, all_pooled)
    grad_wb = lax.psum(local_terms, "space") * scale_b
    wide = grad_pooled.astype(jnp.float32)
    upsampled = jnp.broadcast_to(
        wide[:, :, None, :, None, :, None], (chans, sx // 2, 2, sy // 2, 2, sz // 2, 2)
    ).reshape(chans, sx, sy, sz)
    grad_pre = jnp.where(fine > 0.0, upsampled * 0.125, 0.0).astype(jnp.bfloat16)
    rimmed_pre = with_halo(grad_pre, (("filt", 2), ("space", 1)), 1)
    padded_pre = jnp.pad(rimmed_pre, ((0, 0), (0, 0), (0, 0), (1, 1)))
    grad_input = input_grad(padded_pre, weight_a, (sx, sy, sz)).astype(jnp.bfloat16)
    grad_wa = lax.psum(weight_grad(padded_pre, activation), ("filt", "space")) * scale_a
    return (grad_input, grad_wa, grad_wb)


def solution(mesh):
    placed = (
        P(None, "space", "filt", None),
        P(None, "space", "filt", None),
        P("filt", "space", None, None),
        P(),
        P(None, "filt", None),
    )
    return jax.shard_map(
        per_device,
        mesh=mesh,
        in_specs=placed,
        out_specs=(P(None, "space", "filt", None), P(), P(None, "filt", None)),
        check_vma=False,
    )
```

profile of v0, /device:TPU:1, one launch (start us, length us, event | category | flops | bytes accessed | tf_op | source)
XLA Modules:
  0.0 562.4 jit_solution(6717497816871155632)
XLA Ops:
  8.3 4.4 collective-permute-start
  12.7 1.3 collective-permute-start.1
  14.0 1.4 fusion.111
  16.0 1.7 reduce_sum.18
  18.0 18.7 %all-gather = bf16[32,64,128]{2,0,1:T(8,128)(2,1)S(1)} all-gather(bf16[32,8,128]{2,0,1:T(8,128)(2,1)S(1)} %copy.260), channel_id=2, replica_groups=mesh['filt'=8,'space'=32] {'filt'}, dimensions={1}, use_global_device_ids=true | all-gather | bytes 589824 | tf_op jit(solution)/shard_map/all_gather | solution.py:82
  51.9 1.3 fusion.10
  55.5 133.4 %psum.15 = f32[27,8,32]{2,1,0:T(8,128)S(1)} all-reduce(f32[27,8,32]{2,1,0:T(8,128)S(1)} %fusion.84), channel_id=1, replica_groups=mesh['filt'=8,'space'=32] {'space'}, use_global_device_ids=true, to_apply=%region_4.5 | all-reduce | flops 6912 | bytes 55296 | tf_op jit(solution)/shard_map/psum | solution.py:84
  192.2 30.3 %collective-permute-start.2 = (bf16[32,2,1,256]{3,0,2,1:T(8,128)(2,1)S(1)}, bf16[32,2,1,256]{3,0,2,1:T(8,128)(2,1)S(1)}, u32[]{:S(2)}, u32[]{:S(2)}) collective-permute-start(bf16[32,2,1,256]{3,0,2,1:T(8,128)(2,1)S(1)} %get-tuple-element.19), channel_id=1, source_target_pairs={{0,32},{32,64},{64,96},{96,128},{128,160},{160,192},{192,224},{1,3... | collective-permute-start | bytes 98312 | tf_op jit(solution)/shard_map/ppermute | solution.py:17
  222.6 1.9 collective-permute-start.3
  225.5 3.3 collective-permute-done.3
  228.9 1.3 collective-permute-start.4
  230.2 1.3 collective-permute-start.5
  231.5 2.1 fusion.128
  233.6 2.0 fusion.124
  235.6 4.6 collective-permute-done.5
  240.4 2.0 fusion.132
  242.5 2.0 fusion.134
  244.5 2.1 fusion.136
  246.5 1.6 select_maximum_fusion
  248.1 1.3 fusion.158
  249.4 1.3 fusion.161
  250.8 1.3 fusion.164
  252.1 1.3 fusion.167
  253.4 1.3 fusion.170
  254.8 1.3 fusion.173
  256.1 1.4 fusion.176
  257.5 1.3 fusion.179
  258.8 1.3 convolution_bitcast_fusion.1
  260.1 1.3 convolution_bitcast_fusion.4
  261.4 1.4 convolution_bitcast_fusion.7
  262.8 1.3 convolution_bitcast_fusion
  264.1 1.4 convolution_bitcast_fusion.2
  265.5 1.3 convolution_bitcast_fusion.3
  266.8 1.4 convolution_bitcast_fusion.5
  268.2 1.4 convolution_bitcast_fusion.6
  269.5 1.3 convolution_bitcast_fusion.8
  270.9 1.3 convolution_bitcast_fusion.9
  272.2 1.4 fusion.153
  273.5 1.2 fusion.83
  277.0 1.2 fusion.81
  280.4 1.2 fusion.79
  283.8 1.2 fusion.77
  287.2 1.2 fusion.75
  296.4 1.4 fusion.69
  304.8 5.6 fusion.54
  312.9 1.5 fusion.56
  315.5 238.3 %all-reduce.4.cloned.1.call-done = f32[27,32,32]{2,1,0:T(8,128)} async-done(((f32[27,32,32]{2,1,0:T(8,128)}), f32[27,32,32]{2,1,0:T(8,128)}) %all-reduce.4.cloned.1.call-update) | async-done | bytes 110608 | tf_op jit(solution)/shard_map/psum | solution.py:93
  553.8 1.8 broadcast_multiply_fusion
  (135 shorter events, 51.4 us)
Async XLA Ops:
  7.2 266.4 %copy-start = (bf16[32,2,16,256]{3,2,1,0:T(8,128)(2,1)S(1)}, bf16[32,2,16,256]{3,2,1,0:T(8,128)(2,1)}, u32[]{:S(2)}) copy-start(bf16[32,2,16,256]{3,2,1,0:T(8,128)(2,1)} %param.5) | copy-start | bytes 1572868
  7.2 182.4 %reduce-scatter.2.cloned.1.call-start = ((), (), s32[]{:S(2)}) async-start(), calls=%async_computation.1 | async-start | bytes 1179648 | tf_op jit(solution)/shard_map/reduce_scatter | solution.py:79
  8.3 28.4 %collective-permute-start = (bf16[8,1,64,128]{3,0,2,1:T(8,128)(2,1)S(1)}, bf16[8,1,64,128]{3,0,2,1:T(8,128)(2,1)S(1)}, u32[]{:S(2)}, u32[]{:S(2)}) collective-permute-start(bf16[8,1,64,128]{3,0,2,1:T(8,128)(2,1)S(1)} %copy.198), channel_id=1, source_target_pairs={{0,1},{1,2},{2,3},{3,4},{4,5},{5,6},{6,7},{7,8},{8,9},{9,10},{10,1... | collective-permute-start | bytes 393224 | tf_op jit(solution)/shard_map/ppermute | solution.py:17
  12.7 24.0 %collective-permute-start.1 = (bf16[8,1,64,128]{3,0,2,1:T(8,128)(2,1)S(1)}, bf16[8,1,64,128]{3,0,2,1:T(8,128)(2,1)S(1)}, u32[]{:S(2)}, u32[]{:S(2)}) collective-permute-start(bf16[8,1,64,128]{3,0,2,1:T(8,128)(2,1)S(1)} %copy.198), channel_id=1, source_target_pairs={{1,0},{2,1},{3,2},{4,3},{5,4},{6,5},{7,6},{8,7},{9,8},{10,9},{11,1... | collective-permute-start | bytes 393224 | tf_op jit(solution)/shard_map/ppermute | solution.py:19
  17.7 19.3 %copy-start.16 = (bf16[27,8,32]{2,1,0:T(8,128)(2,1)S(1)}, bf16[27,8,32]{2,1,0:T(8,128)(2,1)}, u32[]{:S(2)}) copy-start(bf16[27,8,32]{2,1,0:T(8,128)(2,1)} %param.9) | copy-start | bytes 41476
  41.2 1.5 copy-start.14
  53.2 500.5 %all-reduce.4.cloned.1.call-start = ((), (), s32[]{:S(2)}) async-start(), calls=%async_computation.2 | async-start | bytes 884736 | tf_op jit(solution)/shard_map/psum | solution.py:93
  55.5 136.3 %copy-start.13 = (bf16[32,2,16,256]{3,2,1,0:T(8,128)(2,1)S(1)}, bf16[32,2,16,256]{3,2,1,0:T(8,128)(2,1)}, u32[]{:S(2)}) copy-start(bf16[32,2,16,256]{3,2,1,0:T(8,128)(2,1)} %param.6) | copy-start | bytes 1572868
  192.2 33.3 %collective-permute-start.2 = (bf16[32,2,1,256]{3,0,2,1:T(8,128)(2,1)S(1)}, bf16[32,2,1,256]{3,0,2,1:T(8,128)(2,1)S(1)}, u32[]{:S(2)}, u32[]{:S(2)}) collective-permute-start(bf16[32,2,1,256]{3,0,2,1:T(8,128)(2,1)S(1)} %get-tuple-element.19), channel_id=1, source_target_pairs={{0,32},{32,64},{64,96},{96,128},{128,160},{160,192},{192,224},{1,3... | collective-permute-start | bytes 98312 | tf_op jit(solution)/shard_map/ppermute | solution.py:17
  222.6 6.2 %collective-permute-start.3 = (bf16[32,2,1,256]{3,0,2,1:T(8,128)(2,1)S(1)}, bf16[32,2,1,256]{3,0,2,1:T(8,128)(2,1)S(1)}, u32[]{:S(2)}, u32[]{:S(2)}) collective-permute-start(bf16[32,2,1,256]{3,0,2,1:T(8,128)(2,1)S(1)} %get-tuple-element.20), channel_id=1, source_target_pairs={{32,0},{64,32},{96,64},{128,96},{160,128},{192,160},{224,192},{33,... | collective-permute-start | bytes 98312 | tf_op jit(solution)/shard_map/ppermute | solution.py:19
  228.9 6.7 %collective-permute-start.4 = (bf16[32,1,18,256]{3,0,2,1:T(8,128)(2,1)S(1)}, bf16[32,1,18,256]{3,0,2,1:T(8,128)(2,1)S(1)}, u32[]{:S(2)}, u32[]{:S(2)}) collective-permute-start(bf16[32,1,18,256]{3,0,2,1:T(8,128)(2,1)S(1)} %get-tuple-element.17), channel_id=1, source_target_pairs={{0,1},{1,2},{2,3},{3,4},{4,5},{5,6},{6,7},{7,8},{8,9},{9,10},{10,1... | collective-permute-start | bytes 884744 | tf_op jit(solution)/shard_map/ppermute | solution.py:17
  230.2 10.0 %collective-permute-start.5 = (bf16[32,1,18,256]{3,0,2,1:T(8,128)(2,1)S(1)}, bf16[32,1,18,256]{3,0,2,1:T(8,128)(2,1)S(1)}, u32[]{:S(2)}, u32[]{:S(2)}) collective-permute-start(bf16[32,1,18,256]{3,0,2,1:T(8,128)(2,1)S(1)} %get-tuple-element.18), channel_id=1, source_target_pairs={{1,0},{2,1},{3,2},{4,3},{5,4},{6,5},{7,6},{8,7},{9,8},{10,9},{11,1... | collective-permute-start | bytes 884744 | tf_op jit(solution)/shard_map/ppermute | solution.py:19
  246.5 1.6 copy-start.15
  304.6 5.7 %copy-start.1 = (f32[2,16,256,32]{2,3,1,0:T(8,128)S(1)}, f32[2,16,256,32]{2,3,1,0:T(8,128)}, u32[]{:S(2)}) copy-start(f32[2,16,256,32]{2,3,1,0:T(8,128)} %fusion.124) | copy-start | bytes 3145732
  304.6 5.7 %copy-start.2 = (f32[32,2,16,256]{3,0,2,1:T(8,128)S(1)}, f32[32,2,16,256]{3,0,2,1:T(8,128)}, u32[]{:S(2)}) copy-start(f32[32,2,16,256]{3,0,2,1:T(8,128)} %convolution_bitcast_fusion.1) | copy-start | bytes 3145732
  304.7 5.7 %copy-start.3 = (f32[32,2,16,256]{3,0,2,1:T(8,128)S(1)}, f32[32,2,16,256]{3,0,2,1:T(8,128)}, u32[]{:S(2)}) copy-start(f32[32,2,16,256]{3,0,2,1:T(8,128)} %convolution_bitcast_fusion.4) | copy-start | bytes 3145732
  304.7 5.8 %copy-start.4 = (f32[32,2,16,256]{3,0,2,1:T(8,128)S(1)}, f32[32,2,16,256]{3,0,2,1:T(8,128)}, u32[]{:S(2)}) copy-start(f32[32,2,16,256]{3,0,2,1:T(8,128)} %convolution_bitcast_fusion.7) | copy-start | bytes 3145732
  304.7 6.1 %copy-start.5 = (f32[32,2,16,256]{3,0,2,1:T(8,128)S(1)}, f32[32,2,16,256]{3,0,2,1:T(8,128)}, u32[]{:S(2)}) copy-start(f32[32,2,16,256]{3,0,2,1:T(8,128)} %convolution_bitcast_fusion) | copy-start | bytes 3145732
  304.7 6.4 %copy-start.6 = (f32[32,2,16,256]{3,0,2,1:T(8,128)S(1)}, f32[32,2,16,256]{3,0,2,1:T(8,128)}, u32[]{:S(2)}) copy-start(f32[32,2,16,256]{3,0,2,1:T(8,128)} %convolution_bitcast_fusion.2) | copy-start | bytes 3145732
  304.7 6.7 %copy-start.7 = (f32[32,2,16,256]{3,0,2,1:T(8,128)S(1)}, f32[32,2,16,256]{3,0,2,1:T(8,128)}, u32[]{:S(2)}) copy-start(f32[32,2,16,256]{3,0,2,1:T(8,128)} %convolution_bitcast_fusion.3) | copy-start | bytes 3145732
  304.7 7.0 %copy-start.8 = (f32[32,2,16,256]{3,0,2,1:T(8,128)S(1)}, f32[32,2,16,256]{3,0,2,1:T(8,128)}, u32[]{:S(2)}) copy-start(f32[32,2,16,256]{3,0,2,1:T(8,128)} %convolution_bitcast_fusion.5) | copy-start | bytes 3145732
  304.7 7.3 %copy-start.9 = (f32[32,2,16,256]{3,0,2,1:T(8,128)S(1)}, f32[32,2,16,256]{3,0,2,1:T(8,128)}, u32[]{:S(2)}) copy-start(f32[32,2,16,256]{3,0,2,1:T(8,128)} %convolution_bitcast_fusion.6) | copy-start | bytes 3145732
  304.7 7.6 %copy-start.10 = (f32[32,2,16,256]{3,0,2,1:T(8,128)S(1)}, f32[32,2,16,256]{3,0,2,1:T(8,128)}, u32[]{:S(2)}) copy-start(f32[32,2,16,256]{3,0,2,1:T(8,128)} %convolution_bitcast_fusion.8) | copy-start | bytes 3145732
  304.7 7.9 %copy-start.11 = (f32[32,2,16,256]{3,0,2,1:T(8,128)S(1)}, f32[32,2,16,256]{3,0,2,1:T(8,128)}, u32[]{:S(2)}) copy-start(f32[32,2,16,256]{3,0,2,1:T(8,128)} %convolution_bitcast_fusion.9) | copy-start | bytes 3145732
  304.7 8.2 %copy-start.12 = (f32[2,16,256,32]{2,3,1,0:T(8,128)S(1)}, f32[2,16,256,32]{2,3,1,0:T(8,128)}, u32[]{:S(2)}) copy-start(f32[2,16,256,32]{2,3,1,0:T(8,128)} %fusion.153) | copy-start | bytes 3145732
Sparse Core Ops, SparseCore 0:
  53.4 39.5 reduce-scatter.1
  304.8 248.9 all-reduce.3
where the time goes:
time: 563 us; the launch traced here: 562 us
  waiting for transfers between devices  246 us (44%)
  blocking collectives  152 us (27%)
  matrix products  92.9 us (17%)
  starting transfers between devices  40.6 us (7%)
  between operations  14.6 us (3%)
  other arithmetic  9.2 us (2%)
  local copies, waits for them, and re-layouts  6.87 us (1%)
    psum x1, waiting for transfers between devices, per_device(): lax.psum(weight_grad(padded_pre, activation), ('filt', 'space')) * scale_a  238 us
    psum x1, blocking collectives, per_device(): grad_wb = lax.psum(local_terms, 'space') * scale_b  133 us
    dot_general x54, matrix products, input_grad(): jnp.einsum('oi,oxyz->ixyz', weight[index], piece, preferred_element_type=...  54.2 us
    dot_general x54, matrix products, weight_grad(): jnp.einsum('oxyz,ixyz->oi', piece, field, preferred_element_type=jnp.floa...  38.8 us
    ppermute x3, starting transfers between devices, with_halo(): lax.ppermute(tail, axis, [(i, (i + 1) % count) for i in range(ends)])  36 us
    all_gather x1, blocking collectives, per_device(): all_pooled = lax.all_gather(pooled, 'filt', axis=2, tiled=True)  18.7 us
  transfers between devices with their start and end apart: 8, of which 3 were waited for; matrix products, arithmetic and copies ran while one was open for 4% of the time, Pallas kernels for 0%

commit v1 on v0

v1 whole, which is shorter than its diff:
```python
import math

import jax
import jax.numpy as jnp
from jax import lax
from jax.experimental import pallas as pl
from jax.experimental.pallas import tpu as pltpu
from jax.sharding import PartitionSpec as P

BF = jnp.bfloat16
F32 = jnp.float32
NF = 8
ROWS = 8
NXY = 16


def shifted(values, step):
    width = values.shape[-1]
    axis = values.ndim - 1
    lane = lax.broadcasted_iota(jnp.int32, values.shape, axis)
    rolled = pltpu.roll(values, step % width, axis)
    edge = 0 if step == 1 else width - 1
    return jnp.where(lane == edge, 0.0, rolled)


def kernel(
    gout,
    pre,
    act,
    wa0,
    wb0,
    up,
    down,
    out,
    gwa_out,
    gwb_out,
    grid_b,
    wb_all,
    tb,
    ta,
    prh,
    gpc,
    gp,
    act3,
    racc,
    gwb,
    rb1,
    rb2,
    sb,
    fin,
    gwa,
    ra1,
    ra2,
    ra3,
    sa,
    s1,
    r1,
    sw,
    rw,
    sp,
    rp,
    sc,
    rc,
    sb1,
    qb1,
    sb2,
    qb2,
    sb3,
    qb3,
    sa1,
    qa1,
    sa2,
    qa2,
    sa3,
    qa3,
):
    f = lax.axis_index("filt")
    p = lax.axis_index("space")
    ns = lax.axis_size("space")
    xy = p // 2
    zl = p % 2

    def fmod(v):
        return lax.rem(v + NF, NF)

    def smod(v):
        return lax.rem(v + ns, ns)

    def xymod(v):
        return lax.rem(v + NXY, NXY)

    def send(src, dst, ss, rs, tf, tp):
        pltpu.make_async_remote_copy(
            src_ref=src,
            dst_ref=dst,
            send_sem=ss,
            recv_sem=rs,
            device_id={"filt": tf, "space": tp},
            device_id_type=pl.DeviceIdType.MESH,
        ).start()

    def wait(ref, sem):
        pltpu.make_async_copy(ref, ref, sem).wait()

    barrier = pltpu.get_barrier_semaphore()

    def greet(tf, tp):
        pl.semaphore_signal(
            barrier,
            inc=1,
            device_id={"filt": tf, "space": tp},
            device_id_type=pl.DeviceIdType.MESH,
        )

    @pl.loop(0, NF)
    def _(j):
        greet(fmod(f + j), smod(p - 1))
        greet(fmod(f + j), smod(p + 1))

    @pl.loop(1, NF)
    def _(j):
        greet(fmod(f + j), p)

    @pl.loop(1, NXY)
    def _(j):
        greet(f, xymod(xy + j) * 2 + zl)

    @pl.loop(0, NF)
    def _(j):
        greet(fmod(f + j), xy * 2 + 1 - zl)

    pl.semaphore_wait(barrier, 3 * NF - 1 + NXY - 1 + NF)

    def block(tf):
        return gout.at[pl.ds(pl.multiple_of(tf * (ROWS * 8), 16), (ROWS + 2) * 8)]

    @pl.loop(1, NF)
    def _(j):
        tf = fmod(f + j)
        send(wb0, wb_all.at[f], sw.at[j], rw.at[f], tf, p)
        send(block(tf), grid_b.at[f, 1], s1.at[1, j], r1.at[1, f], tf, p)

    @pl.loop(0, NF)
    def _(j):
        tf = fmod(f + j)
        send(block(tf), grid_b.at[f, 2], s1.at[0, j], r1.at[2, f], tf, smod(p - 1))
        send(block(tf), grid_b.at[f, 0], s1.at[2, j], r1.at[0, f], tf, smod(p + 1))

    pre_moves = (
        (pre.at[0], prh.at[3, pl.ds(1, 16)], 0, -1),
        (pre.at[1], prh.at[0, pl.ds(1, 16)], 0, 1),
        (pre.at[pl.ds(0, 2), 0], prh.at[pl.ds(1, 2), 17], -1, 0),
        (pre.at[pl.ds(0, 2), 15], prh.at[pl.ds(1, 2), 0], 1, 0),
        (pre.at[0, 0], prh.at[3, 17], -1, -1),
        (pre.at[0, 15], prh.at[3, 0], 1, -1),
        (pre.at[1, 0], prh.at[0, 17], -1, 1),
        (pre.at[1, 15], prh.at[0, 0], 1, 1),
    )
    for n, (src, dst, df, dp) in enumerate(pre_moves):
        send(src, dst, sp.at[n], rp.at[n], fmod(f + df), smod(p + dp))

    own = block(f)
    grid_b[f, 1] = own[...]
    grid_b[:, 3] = jnp.zeros((NF,) + grid_b.shape[2:], BF)
    wb_all[f] = wb0[...]
    prh[1:3, 1:17] = pre[...]

    wide_a = wa0[...].astype(F32)
    for n, turn in enumerate((0, 32, 128, 160)):
        ta[n * 96 : n * 96 + 96] = (
            pltpu.roll(wide_a, turn, 1) if turn else wide_a
        ).astype(BF)

    relu = jnp.maximum(pre[...], jnp.zeros((), BF)).reshape(2, ROWS, 2, 32, 256)
    total = jnp.zeros((ROWS * 32, 128), F32)
    for x2 in range(2):
        for y2 in range(2):
            total += jnp.dot(
                relu[x2, :, y2].reshape(ROWS * 32, 256),
                down[...],
                preferred_element_type=F32,
            )
    pooled = (total * 0.125).astype(BF).astype(F32)
    pooled3 = jnp.stack(
        [
            shifted(pooled, 1).astype(BF).reshape(ROWS // 2, 2, 32, 128),
            pooled.astype(BF).reshape(ROWS // 2, 2, 32, 128),
            shifted(pooled, -1).astype(BF).reshape(ROWS // 2, 2, 32, 128),
            jnp.zeros((ROWS // 2, 2, 32, 128), BF),
        ],
        axis=2,
    ).reshape(ROWS // 2, 256, 128)
    pooled_cat = jnp.concatenate([pooled3[b] for b in range(ROWS // 2)], axis=1)

    @pl.loop(0, 8)
    def _(b):
        for x2 in range(2):
            for y2 in range(2):
                slab = act[x2, 2 * b + y2]
                wide = slab.astype(F32)
                base = (x2 * 2 + y2) * 128
                act3[b, base : base + 32] = shifted(wide, 1).astype(BF)
                act3[b, base + 32 : base + 64] = slab
                act3[b, base + 64 : base + 96] = shifted(wide, -1).astype(BF)
                act3[b, base + 96 : base + 128] = jnp.zeros((32, 256), BF)

    racc[...] = jnp.zeros(racc.shape, F32)

    @pl.loop(1, NF)
    def _(j):
        wait(wb_all.at[0], rw.at[fmod(f + j)])

    for n in range(NF):
        wide_b = wb_all[n].astype(F32)
        tb[0:96, n * 128 : n * 128 + 128] = wb_all[n]
        tb[96:192, n * 128 : n * 128 + 128] = pltpu.roll(wide_b, 8, 1).astype(BF)

    @pl.loop(1, NF)
    def _(j):
        wait(grid_b.at[0, 0], r1.at[1, fmod(f + j)])

    @pl.loop(0, NF)
    def _(j):
        wait(grid_b.at[0, 0], r1.at[0, j])
        wait(grid_b.at[0, 0], r1.at[2, j])

    @pl.when(p == 0)
    def _():
        grid_b[:, 0] = jnp.zeros((NF,) + grid_b.shape[2:], BF)

    @pl.when(p == ns - 1)
    def _():
        grid_b[:, 2] = jnp.zeros((NF,) + grid_b.shape[2:], BF)

    g_cat = jnp.concatenate(
        [grid_b[:, :, 16 * b : 16 * b + 32, :].reshape(1024, 128) for b in range(ROWS // 2)],
        axis=1,
    )
    prod = jnp.dot(tb[...], g_cat, preferred_element_type=F32)
    for b in range(ROWS // 2):
        part = prod[:, b * 128 : b * 128 + 128].reshape(2, 3, 32, 128)
        rows = part[:, 1] + shifted(part[:, 0], -1) + shifted(part[:, 2], 1)
        gpc[1, 1 + 2 * b : 3 + 2 * b] = rows.astype(BF)

    coarse_moves = (
        (gpc.at[1, pl.ds(1, ROWS)], gpc.at[2, pl.ds(1, ROWS)], 0, -1),
        (gpc.at[1, pl.ds(1, ROWS)], gpc.at[0, pl.ds(1, ROWS)], 0, 1),
        (gpc.at[1, 1], gpc.at[1, ROWS + 1], -1, 0),
        (gpc.at[1, ROWS], gpc.at[1, 0], 1, 0),
        (gpc.at[1, 1], gpc.at[2, ROWS + 1], -1, -1),
        (gpc.at[1, ROWS], gpc.at[2, 0], 1, -1),
        (gpc.at[1, 1], gpc.at[0, ROWS + 1], -1, 1),
        (gpc.at[1, ROWS], gpc.at[0, 0], 1, 1),
    )
    for n, (src, dst, df, dp) in enumerate(coarse_moves):
        send(src, dst, sc.at[n], rc.at[n], fmod(f + df), smod(p + dp))

    pairs = lax.dot_general(
        g_cat, pooled_cat, (((1,), (1,)), ((), ())), preferred_element_type=F32
    ).reshape(NF, 4, 4, 8, 256)
    folded = pairs[:, :3, :3, :, :128] + pairs[:, :3, 1:, :, 128:]
    folded = jnp.concatenate(
        [folded.reshape(NF, 72, 128), jnp.zeros((NF, 24, 128), F32)], axis=1
    )
    gwb[...] = folded.astype(BF).reshape(2 * NF, 48, 128)

    @pl.loop(1, NXY)
    def _(j):
        k = xymod(xy + j)
        send(gwb.at[k], rb1.at[xy], sb1.at[j], qb1.at[xy], f, k * 2 + zl)

    rb1[xy] = gwb[xy]

    for n, (src, dst, df, dp) in enumerate(coarse_moves):
        wait(dst, rc.at[n])
    for n, (src, dst, df, dp) in enumerate(pre_moves):
        wait(dst, rp.at[n])

    @pl.when(p == 0)
    def _():
        prh[0] = jnp.zeros(prh.shape[1:], BF)

    @pl.when(p == ns - 1)
    def _():
        prh[3] = jnp.zeros(prh.shape[1:], BF)

    @pl.when(f == 0)
    def _():
        prh[:, 0] = jnp.zeros((4, 32, 256), BF)

    @pl.when(f == NF - 1)
    def _():
        prh[:, 17] = jnp.zeros((4, 32, 256), BF)

    for plane in range(3):
        fine = (
            jnp.dot(gpc[plane].reshape(320, 128), up[...], preferred_element_type=F32)
            .astype(BF)
            .reshape(10, 32, 256)
        )
        for xh in ((0,), (1, 2), (3,))[plane]:
            for row in range(10):
                for yh in (2 * row - 1, 2 * row):
                    if 0 <= yh <= 17:
                        gp[xh, yh] = jnp.where(
                            prh[xh, yh] > jnp.zeros((), BF), fine[row], jnp.zeros((), BF)
                        )

    @pl.loop(0, 8)
    def _(b):
        cells = gp[:, pl.ds(2 * b, 4)].reshape(512, 256)
        part = jnp.dot(ta[...], cells, preferred_element_type=F32).reshape(2, 2, 3, 32, 256)
        rows = part[:, :, 1] + shifted(part[:, :, 0], -1) + shifted(part[:, :, 2], 1)
        out[:, pl.ds(2 * b, 2)] = rows.astype(BF)
        racc[...] += lax.dot_general(
            cells, act3[b], (((1,), (1,)), ((), ())), preferred_element_type=F32
        )

    taps = []
    for dx in range(3):
        for dy in range(3):
            term = None
            for x2 in range(2):
                for y2 in range(2):
                    r0 = ((x2 + dx) * 4 + y2 + dy) * 32
                    c0 = (x2 * 2 + y2) * 128
                    piece = racc[r0 : r0 + 32, c0 : c0 + 128]
                    term = piece if term is None else term + piece
            taps.append(term)
    full = jnp.concatenate(taps, axis=0)
    rest = full[216:288]
    tail = jnp.concatenate([pltpu.roll(rest, turn, 1) for turn in (96, 64, 32)], axis=0)
    lane = lax.broadcasted_iota(jnp.int32, (216, 128), 1)
    packed = jnp.where(lane < 96, full[:216], tail)
    packed = jnp.concatenate([packed, jnp.zeros((40, 128), F32)], axis=0)
    gwa[...] = packed.astype(BF).reshape(NXY, 16, 128)

    @pl.loop(1, NXY)
    def _(j):
        k = xymod(xy + j)
        send(gwa.at[k], ra1.at[xy], sa1.at[j], qa1.at[xy], f, k * 2 + zl)

    ra1[xy] = gwa[xy]

    @pl.loop(1, NXY)
    def _(j):
        wait(rb1.at[0], qb1.at[xymod(xy + j)])

    owner = xy // 2
    me2 = f * 2 + zl
    sb[...] = jnp.sum(rb1[...].astype(F32), axis=0).astype(BF)
    for zt in range(2):

        @pl.when((f != owner) | (zl != zt))
        def _():
            send(sb, rb2.at[me2], sb2.at[zt], qb2.at[me2], owner, xy * 2 + zt)

    @pl.loop(1, NXY)
    def _(j):
        wait(ra1.at[0], qa1.at[xymod(xy + j)])

    sa[...] = jnp.sum(ra1[...].astype(F32), axis=0).astype(BF)

    @pl.loop(1, NXY)
    def _(j):
        t = xymod(me2 + j)
        send(sa, ra2.at[me2], sa2.at[j], qa2.at[me2], t // 2, xy * 2 + lax.rem(t, 2))

    ra2[me2] = sa[...]

    half = lax.rem(xy, 2)

    @pl.when(f == owner)
    def _():
        rb2[me2] = sb[...]

        @pl.loop(1, NXY)
        def _(j):
            wait(rb2.at[0], qb2.at[xymod(me2 + j)])

        fin[half] = jnp.sum(rb2[...].astype(F32), axis=0)

        @pl.loop(1, NXY)
        def _(j):
            send(fin.at[half], fin.at[half], sb3.at[j], qb3.at[half], f, xymod(xy + j) * 2 + zl)

    @pl.loop(1, NXY)
    def _(j):
        wait(ra2.at[0], qa2.at[xymod(me2 + j)])

    ra3[xy] = jnp.sum(ra2[...].astype(F32), axis=0).astype(BF)

    @pl.loop(1, NXY)
    def _(j):
        k = xymod(xy + j)
        send(ra3.at[xy], ra3.at[xy], sa3.at[j], qa3.at[xy], f, k * 2 + zl)

    for h in range(2):

        @pl.when(xy != 2 * f + h)
        def _():
            wait(fin.at[h], qb3.at[h])

        gwb_out[h] = fin[h] * (1.0 / math.sqrt(ns * NF * ROWS * 128))

    @pl.loop(1, NXY)
    def _(j):
        wait(ra3.at[0], qa3.at[xymod(xy + j)])

    gwa_out[...] = ra3[...].astype(F32) * (1.0 / math.sqrt(8 * ns * NF * ROWS * 128))

    @pl.loop(1, NF)
    def _(j):
        wait(wb0, sw.at[j])
        wait(grid_b.at[0, 0], s1.at[1, j])

    @pl.loop(0, NF)
    def _(j):
        wait(grid_b.at[0, 0], s1.at[0, j])
        wait(grid_b.at[0, 0], s1.at[2, j])

    for n, (src, dst, df, dp) in enumerate(pre_moves):
        wait(src, sp.at[n])
    for n, (src, dst, df, dp) in enumerate(coarse_moves):
        wait(src, sc.at[n])

    @pl.loop(1, NXY)
    def _(j):
        wait(gwb.at[0], sb1.at[j])
        wait(gwa.at[0], sa1.at[j])
        wait(sa, sa2.at[j])
        wait(ra3.at[0], sa3.at[j])

    for zt in range(2):

        @pl.when((f != owner) | (zl != zt))
        def _():
            wait(sb, sb2.at[zt])

    @pl.when(f == owner)
    def _():
        @pl.loop(1, NXY)
        def _(j):
            wait(fin.at[0], sb3.at[j])


def tap_rows(weight):
    o, i = weight.shape[1:]
    parts = weight.reshape(3, 3, 3, o, i)[::-1, ::-1]
    parts = jnp.transpose(parts, (2, 4, 0, 1, 3))
    parts = jnp.pad(parts, ((0, 0), (0, 0), (0, 1), (0, 1), (0, 0)))
    return parts.reshape(3 * i, 16 * o)


def per_device(activation, preact, grad_out, weight_a, weight_b):
    depth = grad_out.shape[3]
    gout = jnp.pad(jnp.transpose(grad_out[:, 0], (1, 0, 2)), ((1, 1), (0, 0), (0, 0)))
    gout = gout.reshape(-1, depth)
    pre = jnp.transpose(preact, (1, 2, 0, 3))
    act = jnp.transpose(activation, (1, 2, 0, 3))
    fine_of = jnp.arange(2 * depth)[None, :] // 2 == jnp.arange(depth)[:, None]
    up = jnp.where(fine_of, 0.125, 0.0).astype(BF)
    down = fine_of.T.astype(BF)
    vmem = pl.BlockSpec(memory_space=pltpu.VMEM)
    dma = pltpu.SemaphoreType.DMA
    out, gwa, gwb = pl.pallas_call(
        kernel,
        out_shape=(
            jax.ShapeDtypeStruct((2, 16, 32, 256), BF),
            jax.ShapeDtypeStruct((NXY, 16, 128), F32),
            jax.ShapeDtypeStruct((2, 48, 128), F32),
        ),
        in_specs=[vmem] * 7,
        out_specs=(vmem,) * 3,
        scratch_shapes=[
            pltpu.VMEM((NF, 4, 80, 128), BF),
            pltpu.VMEM((NF, 96, 128), BF),
            pltpu.VMEM((192, 1024), BF),
            pltpu.VMEM((384, 512), BF),
            pltpu.VMEM((4, 18, 32, 256), BF),
            pltpu.VMEM((3, 10, 32, 128), BF),
            pltpu.VMEM((4, 18, 32, 256), BF),
            pltpu.VMEM((8, 512, 256), BF),
            pltpu.VMEM((512, 512), F32),
            pltpu.VMEM((NXY, 48, 128), BF),
            pltpu.VMEM((NXY, 48, 128), BF),
            pltpu.VMEM((NXY, 48, 128), BF),
            pltpu.VMEM((48, 128), BF),
            pltpu.VMEM((2, 48, 128), F32),
            pltpu.VMEM((NXY, 16, 128), BF),
            pltpu.VMEM((NXY, 16, 128), BF),
            pltpu.VMEM((NXY, 16, 128), BF),
            pltpu.VMEM((NXY, 16, 128), BF),
            pltpu.VMEM((16, 128), BF),
            dma((3, NF)),
            dma((3, NF)),
            dma((NF,)),
            dma((NF,)),
            dma((8,)),
            dma((8,)),
            dma((8,)),
            dma((8,)),
            dma((NXY,)),
            dma((NXY,)),
            dma((2,)),
            dma((NXY,)),
            dma((NXY,)),
            dma((2,)),
            dma((NXY,)),
            dma((NXY,)),
            dma((NXY,)),
            dma((NXY,)),
            dma((NXY,)),
            dma((NXY,)),
        ],
        compiler_params=pltpu.CompilerParams(
            collective_id=0, has_side_effects=True, vmem_limit_bytes=48 * 1024 * 1024
        ),
    )(gout, pre, act, tap_rows(weight_a), tap_rows(weight_b), up, down)
    grad_input = jnp.transpose(out, (2, 0, 1, 3))
    packed = gwa.reshape(256, 128)
    rest = packed[:216, 96:].reshape(3, 72, 32).transpose(1, 0, 2).reshape(72, 96)
    full = jnp.concatenate([packed[:216, :96], rest], axis=0)
    full = full.reshape(3, 3, 32, 3, 32)[::-1, ::-1]
    grad_wa = jnp.transpose(full, (0, 1, 3, 2, 4)).reshape(27, 32, 32)
    part = gwb.reshape(96, 128)[:72, :96].reshape(3, 3, 8, 3, 32)[::-1, ::-1]
    grad_wb = jnp.transpose(part, (0, 1, 3, 2, 4)).reshape(27, 8, 32)
    return (grad_input, grad_wa, grad_wb)


def solution(mesh):
    placed = (
        P(None, "space", "filt", None),
        P(None, "space", "filt", None),
        P("filt", "space", None, None),
        P(),
        P(None, "filt", None),
    )
    return jax.shard_map(
        per_device,
        mesh=mesh,
        in_specs=placed,
        out_specs=(P(None, "space", "filt", None), P(), P(None, "filt", None)),
        check_vma=False,
    )
```

time: 563 us -> 77.2 us (0.14)
  waiting for transfers between devices: 246 us -> 0 us
  blocking collectives: 152 us -> 0 us
  matrix products: 92.9 us -> 0 us
  Pallas kernels: 0 us -> 67.5 us
  starting transfers between devices: 40.6 us -> 0 us
  between operations: 14.6 us -> 0.84 us
  other arithmetic: 9.2 us -> 0.14 us
    psum x1 -> x0, waiting for transfers between devices: 238 us -> none  [per_device(): lax.psum(weight_grad(padded_pre, activation), ('filt', 'space')) * scale_a]
    psum x1 -> x0, blocking collectives: 133 us -> none  [per_device(): grad_wb = lax.psum(local_terms, 'space') * scale_b]
    dot_general x108 -> x0, matrix products: 92.9 us -> none  [the longest x54 54.2 us: input_grad(): jnp.einsum('oi,oxyz->ixyz', weight[index], piece, preferred_element_type=...]
    pallas_call x0 -> x1, Pallas kernels: none -> 67.5 us  [per_device(): pl.pallas_call(kernel, out_shape=(jax.ShapeDtypeStruct((2, 16, 32, 256),...]
    ppermute x6 -> x0, starting transfers between devices: 40.5 us -> none  [the longest x3 36 us: with_halo(): lax.ppermute(tail, axis, [(i, (i + 1) % count) for i in range(ends)])]
    all_gather x1 -> x0, blocking collectives: 18.7 us -> none  [per_device(): all_pooled = lax.all_gather(pooled, 'filt', axis=2, tiled=True)]
    ppermute x6 -> x0, waiting for transfers between devices: 7.87 us -> none  [the longest x3 7.86 us: with_halo(): lax.ppermute(head, axis, [((i + 1) % count, i) for i in range(ends)])]
  transfers between devices with their start and end apart: 8 -> 0, of which waited for: 3 -> 0; matrix products, arithmetic and copies ran while one was open for 4% -> 0% of each run, Pallas kernels for 0% -> 0%
where the time goes in v1:
time: 77.2 us; the launch traced here: 77 us
  Pallas kernels  67.5 us (87%)
  local copies, waits for them, and re-layouts  8.52 us (11%)
  between operations  0.84 us (1%)
    pallas_call x1, Pallas kernels, per_device(): pl.pallas_call(kernel, out_shape=(jax.ShapeDtypeStruct((2, 16, 32, 256),...  67.5 us
    unnamed x12, local copies, waits for them, and re-layouts  4.03 us

profile of v1, /device:TPU:1, one launch (start us, length us, event | category | flops | bytes accessed | tf_op | source)
XLA Modules:
  0.0 77.0 jit_solution(10711779805262110661)
XLA Ops:
  0.6 0.0 copy-start.4
  0.7 0.1 fusion.down
  0.8 0.7 copy-done.4
  1.6 0.0 copy-start.3
  1.6 0.1 reshape.86
  1.7 0.1 copy.31.wb0
  1.8 0.7 copy-done.3
  2.5 0.0 copy-start.2
  2.5 0.1 copy.37
  2.6 0.8 %copy-done.2 = bf16[27,32,32]{2,1,0:T(8,128)(2,1)S(1)} copy-done((bf16[27,32,32]{2,1,0:T(8,128)(2,1)S(1)}, bf16[27,32,32]{2,1,0:T(8,128)(2,1)}, u32[]{:S(2)}) %copy-start.2) | copy-done | bytes 55320
  3.4 0.2 copy.29
  3.6 0.7 rev.12
  4.3 0.0 copy-start
  4.3 0.0 copy-start.1
  4.3 0.2 pad.13
  4.5 0.3 reshape.84.wa0
  4.8 0.5 copy-done
  5.4 0.2 copy-done.1
  5.5 0.6 copy_bitcast_fusion
  6.1 67.5 %shard_map.76 = (bf16[2,16,32,256]{3,2,1,0:T(8,128)(2,1)S(1)}, f32[16,16,128]{2,1,0:T(8,128)S(1)}, f32[2,48,128]{2,1,0:T(8,128)S(1)}) custom-call(bf16[528,128]{1,0:T(8,128)(2,1)S(1)} %pad_bitcast_fusion.gout, bf16[2,16,32,256]{3,2,1,0:T(8,128)(2,1)S(1)} %get-tuple-element.19.pre, bf16[2,16,32,256]{3,2,1,0:T(8,128)(2,1)S(1)} %get-tuple-element.18.act, ...), custom_call_target="tpu_custom_call" | custom-call | tf_op jit(solution)/shard_map/pallas_call | solution.py:466
  73.6 1.1 %copy.36 = bf16[32,2,16,256]{3,2,1,0:T(8,128)(2,1)} copy(bf16[32,2,16,256]{3,0,2,1:T(8,128)(2,1)S(1)} %bitcast.29) | data formatting | bytes 1048576
  74.7 0.1 reshape.93
  74.9 0.7 copy.35
  75.5 0.1 slice.13
  75.6 0.1 copy.32
  75.7 0.1 copy.33
  75.8 0.2 reshape.90
  76.1 0.1 reverse_bitcast_fusion
  76.2 0.8 %copy.34 = f32[3,3,3,32,32]{4,3,2,1,0:T(8,128)} copy(f32[3,3,3,32,32]{4,2,3,1,0:T(4,128)S(1)} %reverse_bitcast_fusion) | data formatting | bytes 221184 | tf_op jit(solution)/shard_map/transpose | solution.py:525
  (10 shorter events, 0.2 us)
Async XLA Ops:
  0.6 0.8 %copy-start.4 = (bf16[27,8,32]{2,1,0:T(8,128)(2,1)S(1)}, bf16[27,8,32]{2,1,0:T(8,128)(2,1)}, u32[]{:S(2)}) copy-start(bf16[27,8,32]{2,1,0:T(8,128)(2,1)} %param.9) | copy-start | bytes 41476
  1.6 0.9 %copy-start.3 = (bf16[8,1,64,128]{3,2,1,0:T(8,128)(2,1)S(1)}, bf16[8,1,64,128]{3,2,1,0:T(8,128)(2,1)}, u32[]{:S(2)}) copy-start(bf16[8,1,64,128]{3,2,1,0:T(8,128)(2,1)} %param.7) | copy-start | bytes 393220
  2.5 0.9 %copy-start.2 = (bf16[27,32,32]{2,1,0:T(8,128)(2,1)S(1)}, bf16[27,32,32]{2,1,0:T(8,128)(2,1)}, u32[]{:S(2)}) copy-start(bf16[27,32,32]{2,1,0:T(8,128)(2,1)} %param.8) | copy-start | bytes 165892
  4.3 1.0 %copy-start = (bf16[32,2,16,256]{3,2,1,0:T(8,128)(2,1)S(1)}, bf16[32,2,16,256]{3,2,1,0:T(8,128)(2,1)}, u32[]{:S(2)}) copy-start(bf16[32,2,16,256]{3,2,1,0:T(8,128)(2,1)} %param.5) | copy-start | bytes 1572868
  4.3 1.2 %copy-start.1 = (bf16[32,2,16,256]{3,2,1,0:T(8,128)(2,1)S(1)}, bf16[32,2,16,256]{3,2,1,0:T(8,128)(2,1)}, u32[]{:S(2)}) copy-start(bf16[32,2,16,256]{3,2,1,0:T(8,128)(2,1)} %param.6) | copy-start | bytes 1572868

commit v2 on v1

v2 whole, which is shorter than its diff:
```python
import math

import jax
import jax.numpy as jnp
from jax import lax
from jax.experimental import pallas as pl
from jax.experimental.pallas import tpu as pltpu
from jax.sharding import PartitionSpec as P

BF = jnp.bfloat16
F32 = jnp.float32
NF = 8
ROWS = 8
NXY = 16
PRE_AT = 5


def shifted(values, step):
    width = values.shape[-1]
    axis = values.ndim - 1
    lane = lax.broadcasted_iota(jnp.int32, values.shape, axis)
    rolled = pltpu.roll(values, step % width, axis)
    edge = 0 if step == 1 else width - 1
    return jnp.where(lane == edge, 0.0, rolled)


def kernel(
    gout_h,
    pre_h,
    act_h,
    wa_h,
    wb_h,
    out_t,
    gwa_out,
    gwb_out,
    graw,
    praw,
    araw,
    waraw,
    wbraw,
    gsrc,
    wb0,
    grid_b,
    wb_all,
    tb,
    ta,
    prh,
    pool,
    pool2,
    pcat,
    gpo,
    gpc,
    gp,
    actt,
    act3,
    racc,
    out_v,
    gwb,
    rb1,
    rb2,
    sb,
    fin,
    gwa,
    ra1,
    ra2,
    ra3,
    sa,
    sin,
    s1,
    r1,
    sf,
    rf,
    sw,
    rw,
    sx,
    spool,
    rpool,
    sp,
    rp,
    sc,
    rc,
    sb1,
    qb1,
    sb2,
    qb2,
    sb3,
    qb3,
    sa1,
    qa1,
    sa2,
    qa2,
    sa3,
    qa3,
):
    f = lax.axis_index("filt")
    p = lax.axis_index("space")
    ns = lax.axis_size("space")
    xy = p // 2
    zl = p % 2
    me2 = f * 2 + zl

    def fmod(v):
        return lax.rem(v + NF, NF)

    def smod(v):
        return lax.rem(v + ns, ns)

    def xymod(v):
        return lax.rem(v + NXY, NXY)

    def send(src, dst, ss, rs, tf, tp):
        pltpu.make_async_remote_copy(
            src_ref=src,
            dst_ref=dst,
            send_sem=ss,
            recv_sem=rs,
            device_id={"filt": tf, "space": tp},
            device_id_type=pl.DeviceIdType.MESH,
        ).start()

    def wait(ref, sem):
        pltpu.make_async_copy(ref, ref, sem).wait()

    barrier = pltpu.get_barrier_semaphore()

    def greet(tf, tp):
        pl.semaphore_signal(
            barrier,
            inc=1,
            device_id={"filt": tf, "space": tp},
            device_id_type=pl.DeviceIdType.MESH,
        )

    @pl.loop(1, NXY)
    def _(j):
        t = xymod(me2 + j)
        greet(t // 2, xy * 2 + lax.rem(t, 2))

    @pl.loop(1, NXY)
    def _(j):
        greet(f, xymod(xy + j) * 2 + zl)

    cross = xymod(xy + 2 * zl - 1) * 2 + 1 - zl
    greet(f, cross)
    greet(fmod(f - 1), cross)
    greet(fmod(f + 1), cross)
    greet(fmod(f - 1), xymod(xy + 1) * 2 + zl)
    greet(fmod(f + 1), xymod(xy - 1) * 2 + zl)

    loads = [
        pltpu.make_async_copy(src, dst, sin.at[n])
        for n, (src, dst) in enumerate(
            ((gout_h, graw), (wb_h, wbraw), (pre_h, praw), (wa_h, waraw), (act_h, araw))
        )
    ]
    for load in loads:
        load.start()

    def selection(rows, per, high, low):
        row = lax.broadcasted_iota(jnp.int32, (rows, 4 * high), 0)
        col = lax.broadcasted_iota(jnp.int32, (rows, 4 * high), 1)
        tap = lax.shift_right_logical(row, per.bit_length() - 1)
        dx = lax.shift_right_logical(tap * 11, 5)
        dy = tap - 3 * dx
        place = (2 - dx) * high + (2 - dy) * low + (row - tap * per)
        return jnp.where(col == place, 1.0, 0.0).astype(BF)

    def arranged(raw, per, high, low):
        place = selection(9 * per, per, high, low)
        parts = []
        for dz in range(3):
            tall = jnp.concatenate([raw[3 * k + dz].astype(F32) for k in range(9)], axis=0)
            parts.append(
                lax.dot_general(
                    tall.astype(BF),
                    place,
                    (((0,), (0,)), ((), ())),
                    preferred_element_type=F32,
                )
            )
        return jnp.concatenate(parts, axis=0)

    loads[0].wait()
    rows = jnp.swapaxes(graw[...].astype(F32), 0, 1).reshape(512, 128)
    edge = jnp.zeros((8, 128), F32)
    gsrc[...] = jnp.concatenate([edge, rows, edge], axis=0).astype(BF)
    loads[1].wait()
    wb0[...] = arranged(wbraw, 8, 32, 8).astype(BF)

    pl.semaphore_wait(barrier, 2 * (NXY - 1) + 5)

    core = lax.rem(f, 2)
    sibling = f + 1 - 2 * core

    @pl.loop(1, 4)
    def _(j):
        send(wb0, wb_all.at[f], sw.at[j], rw.at[f], fmod(f + 2 * j), p)

    send(wb0, wb_all.at[f], sx.at[0], rw.at[f], sibling, p)
    wb_all[f] = wb0[...]

    def block(t):
        return gsrc.at[pl.ds(pl.multiple_of(t * 32, 16), 48)]

    @pl.loop(1, NXY)
    def _(j):
        t = xymod(me2 + j)
        send(
            block(t),
            grid_b.at[f, 1 + zl],
            s1.at[j],
            r1.at[me2],
            t // 2,
            xy * 2 + lax.rem(t, 2),
        )

    loads[2].wait()
    for x in range(2):
        turned = jnp.swapaxes(praw[:, x].astype(F32), 0, 1)
        prh[1 + x, 1:17] = turned.astype(BF)

    pre_moves = (
        (prh.at[1, pl.ds(1, 16)], prh.at[3, pl.ds(1, 16)], 0, -1),
        (prh.at[2, pl.ds(1, 16)], prh.at[0, pl.ds(1, 16)], 0, 1),
        (prh.at[pl.ds(1, 2), 1], prh.at[pl.ds(1, 2), 17], -1, 0),
        (prh.at[pl.ds(1, 2), 16], prh.at[pl.ds(1, 2), 0], 1, 0),
        (prh.at[1, 1], prh.at[3, 17], -1, -1),
        (prh.at[1, 16], prh.at[3, 0], 1, -1),
        (prh.at[2, 1], prh.at[0, 17], -1, 1),
        (prh.at[2, 16], prh.at[0, 0], 1, 1),
    )

    def send_pre(first=0, last=8):
        for n in range(first, last):
            src, dst, df, dp = pre_moves[n]
            send(src, dst, sp.at[n], rp.at[n], fmod(f + df), smod(p + dp))

    if PRE_AT == 0:
        send_pre()

    grid_b[f, 1 + zl] = gsrc[pl.ds(pl.multiple_of(me2 * 32, 16), 48)]

    def forward(s):
        sz = lax.rem(s, 2)
        send(
            grid_b.at[s // 2, 1 + sz],
            grid_b.at[s // 2, 3 - 3 * sz],
            sf.at[s],
            rf.at[s],
            f,
            xymod(xy + 2 * sz - 1) * 2 + zl,
        )

    forward(me2)

    fine_row = lax.broadcasted_iota(jnp.int32, (256, 128), 0)
    fine_col = lax.broadcasted_iota(jnp.int32, (256, 128), 1)
    down = jnp.where(lax.shift_right_logical(fine_row, 1) == fine_col, 1.0, 0.0).astype(BF)
    total = jnp.zeros((ROWS * 32, 128), F32)
    for x2 in range(2):
        relu = jnp.maximum(prh[1 + x2, 1:17], jnp.zeros((), BF)).reshape(ROWS, 2, 32, 256)
        for y2 in range(2):
            total += jnp.dot(
                relu[:, y2].reshape(ROWS * 32, 256), down, preferred_element_type=F32
            )
    pool[...] = (total * 0.125).astype(BF).reshape(ROWS, 32, 128)
    send(
        pool.at[pl.ds(4 - 4 * zl, 4)],
        pool2.at[zl],
        spool.at[0],
        rpool.at[0],
        f,
        xy * 2 + 1 - zl,
    )
    pool2[zl] = pool[pl.ds(4 * zl, 4)]

    if PRE_AT == 7:
        send_pre(0, 1)
    @pl.loop(1, 4)
    def _(j):
        s = fmod(f - 2 * j)
        wait(wb0, rw.at[s])
        send(wb_all.at[s], wb_all.at[s], sx.at[j], rw.at[s], sibling, p)

    if PRE_AT == 5:
        send_pre()
    if PRE_AT == 6:
        send_pre(0, 1)
    @pl.loop(1, NXY)
    def _(j):
        s = xymod(me2 - j)
        wait(grid_b.at[0, 0], r1.at[s])
        forward(s)

    if PRE_AT == 1:
        send_pre()
    if PRE_AT in (6, 7):
        send_pre(1, 8)

    loads[3].wait()
    wide_a = arranged(waraw, 32, 128, 32)
    for n, turn in enumerate((0, 32, 128, 160)):
        ta[n * 96 : n * 96 + 96] = (
            pltpu.roll(wide_a, turn, 1) if turn else wide_a
        ).astype(BF)

    @pl.loop(0, 4)
    def _(j):
        wait(wb0, rw.at[2 * j + 1 - core])

    for n in range(NF):
        wide_b = wb_all[n].astype(F32)
        for k, turn in enumerate((0, 8, 32, 40)):
            tb[k * 96 : k * 96 + 96, n * 128 : n * 128 + 128] = (
                pltpu.roll(wide_b, turn, 1) if turn else wide_b
            ).astype(BF)

    @pl.loop(0, NXY)
    def _(j):
        wait(grid_b.at[0, 0], rf.at[j])

    @pl.when(xy == 0)
    def _():
        grid_b[:, 0] = jnp.zeros((NF,) + grid_b.shape[2:], BF)

    @pl.when(xy == NXY - 1)
    def _():
        grid_b[:, 3] = jnp.zeros((NF,) + grid_b.shape[2:], BF)

    g_cat = jnp.concatenate(
        [grid_b[:, :, 16 * b : 16 * b + 32, :].reshape(1024, 128) for b in range(2)], axis=1
    )
    prod = jnp.dot(tb[...], g_cat, preferred_element_type=F32)
    for b in range(2):
        term = prod[:, b * 128 : b * 128 + 128].reshape(2, 2, 3, 32, 128)
        rows = term[:, :, 1] + shifted(term[:, :, 0], -1) + shifted(term[:, :, 2], 1)
        gpo[:, 2 * b : 2 * b + 2] = rows.astype(BF)

    right = xymod(xy + 1) * 2
    left = xymod(xy - 1) * 2 + 1
    step = fmod(f + 2 * zl - 1)
    own_rows = pl.ds(1 + 4 * zl, 4)
    far = 9 - 9 * zl
    both = pl.ds(0, 2)
    coarse_moves = (
        (gpo, gpc.at[pl.ds(zl, 2), own_rows], 0, f, xy * 2 + 1 - zl),
        (gpo.at[1], gpc.at[0, own_rows], 1 + zl, f, right),
        (gpo.at[0], gpc.at[2, own_rows], 1 + zl, f, left),
        (gpo.at[both, 3 * zl], gpc.at[pl.ds(1, 2), far], 3 + zl, step, xy * 2),
        (gpo.at[both, 3 * zl], gpc.at[pl.ds(0, 2), far], 3 + zl, step, xy * 2 + 1),
        (gpo.at[1, 3 * zl], gpc.at[0, far], 5 + zl, step, right),
        (gpo.at[0, 3 * zl], gpc.at[2, far], 5 + zl, step, left),
    )
    for n, (src, dst, slot, tf, tp) in enumerate(coarse_moves):
        send(src, dst, sc.at[n], rc.at[slot], tf, tp)
    gpc[pl.ds(1 - zl, 2), own_rows] = gpo[...]

    wait(pool2.at[0], rpool.at[0])
    mid = pool2[...].reshape(256, 128).astype(F32)
    for k, version in enumerate((shifted(mid, 1), mid, shifted(mid, -1), jnp.zeros_like(mid))):
        version = version.astype(BF).reshape(2, 2, 2, 32, 128)
        for x2 in range(2):
            for b in range(2):
                for y2 in range(2):
                    r0 = (x2 * 2 + y2) * 128 + k * 32
                    pcat[r0 : r0 + 32, b * 128 : b * 128 + 128] = version[x2, b, y2]
    pairs = lax.dot_general(
        g_cat, pcat[...], (((1,), (1,)), ((), ())), preferred_element_type=F32
    ).reshape(NF, 4, 4, 8, 512)
    folded = None
    for x2 in range(2):
        for y2 in range(2):
            c0 = (x2 * 2 + y2) * 128
            term = pairs[:, x2 : x2 + 3, y2 : y2 + 3, :, c0 : c0 + 128]
            folded = term if folded is None else folded + term
    folded = jnp.concatenate(
        [folded.reshape(NF, 72, 128), jnp.zeros((NF, 24, 128), F32)], axis=1
    )
    gwb[...] = folded.astype(BF).reshape(2 * NF, 48, 128)

    @pl.loop(1, NXY)
    def _(j):
        k = xymod(xy + j)
        send(gwb.at[k], rb1.at[xy], sb1.at[j], qb1.at[xy], f, k * 2 + zl)

    rb1[xy] = gwb[xy]

    loads[4].wait()
    for x in range(2):
        actt[x] = jnp.swapaxes(araw[:, x].astype(F32), 0, 1)

    @pl.loop(0, 8)
    def _(b):
        for x2 in range(2):
            for y2 in range(2):
                wide = actt[x2, 2 * b + y2]
                base = (x2 * 2 + y2) * 128
                act3[b, base : base + 32] = shifted(wide, 1).astype(BF)
                act3[b, base + 32 : base + 64] = wide.astype(BF)
                act3[b, base + 64 : base + 96] = shifted(wide, -1).astype(BF)
                act3[b, base + 96 : base + 128] = jnp.zeros((32, 256), BF)

    @pl.loop(1, NXY)
    def _(j):
        wait(rb1.at[0], qb1.at[xymod(xy + j)])

    owner = xy // 2
    sb[...] = jnp.sum(rb1[...].astype(F32), axis=0).astype(BF)
    for zt in range(2):

        @pl.when((f != owner) | (zl != zt))
        def _():
            send(sb, rb2.at[me2], sb2.at[zt], qb2.at[me2], owner, xy * 2 + zt)

    wait(gpo, rc.at[0])
    for n in range(2):
        wait(gpo.at[0], rc.at[1 + n])
        wait(gpo.at[both, 0], rc.at[3 + n])
        wait(gpo.at[0, 0], rc.at[5 + n])
    for n, (src, dst, df, dp) in enumerate(pre_moves):
        wait(dst, rp.at[n])

    @pl.when(p == 0)
    def _():
        prh[0] = jnp.zeros(prh.shape[1:], BF)

    @pl.when(p == ns - 1)
    def _():
        prh[3] = jnp.zeros(prh.shape[1:], BF)

    @pl.when(f == 0)
    def _():
        prh[:, 0] = jnp.zeros((4, 32, 256), BF)

    @pl.when(f == NF - 1)
    def _():
        prh[:, 17] = jnp.zeros((4, 32, 256), BF)

    up_row = lax.broadcasted_iota(jnp.int32, (128, 256), 0)
    up_col = lax.broadcasted_iota(jnp.int32, (128, 256), 1)
    up = jnp.where(lax.shift_right_logical(up_col, 1) == up_row, 0.125, 0.0).astype(BF)
    for plane in range(3):
        fine = (
            jnp.dot(gpc[plane].reshape(320, 128), up, preferred_element_type=F32)
            .astype(BF)
            .reshape(10, 32, 256)
        )
        for xh in ((0,), (1, 2), (3,))[plane]:
            for row in range(10):
                for yh in (2 * row - 1, 2 * row):
                    if 0 <= yh <= 17:
                        gp[xh, yh] = jnp.where(
                            prh[xh, yh] > jnp.zeros((), BF), fine[row], jnp.zeros((), BF)
                        )

    racc[...] = jnp.zeros(racc.shape, F32)

    @pl.loop(0, 8)
    def _(b):
        cells = gp[:, pl.ds(2 * b, 4)].reshape(512, 256)
        racc[...] += lax.dot_general(
            cells, act3[b], (((1,), (1,)), ((), ())), preferred_element_type=F32
        )

    taps = []
    for dx in range(3):
        for dy in range(3):
            term = None
            for x2 in range(2):
                for y2 in range(2):
                    r0 = ((x2 + dx) * 4 + y2 + dy) * 32
                    c0 = (x2 * 2 + y2) * 128
                    piece = racc[r0 : r0 + 32, c0 : c0 + 128]
                    term = piece if term is None else term + piece
            taps.append(term)
    full = jnp.concatenate(taps, axis=0)
    rest = full[216:288]
    tail = jnp.concatenate([pltpu.roll(rest, turn, 1) for turn in (96, 64, 32)], axis=0)
    lane = lax.broadcasted_iota(jnp.int32, (216, 128), 1)
    packed = jnp.where(lane < 96, full[:216], tail)
    packed = jnp.concatenate([packed, jnp.zeros((40, 128), F32)], axis=0)
    gwa[...] = packed.astype(BF).reshape(NXY, 16, 128)

    @pl.loop(1, NXY)
    def _(j):
        k = xymod(xy + j)
        send(gwa.at[k], ra1.at[xy], sa1.at[j], qa1.at[xy], f, k * 2 + zl)

    ra1[xy] = gwa[xy]

    half = lax.rem(xy, 2)

    @pl.when(f == owner)
    def _():
        rb2[me2] = sb[...]

        @pl.loop(1, NXY)
        def _(j):
            wait(rb2.at[0], qb2.at[xymod(me2 + j)])

        fin[half] = jnp.sum(rb2[...].astype(F32), axis=0)

        @pl.loop(1, NXY)
        def _(j):
            send(fin.at[half], fin.at[half], sb3.at[j], qb3.at[half], f, xymod(xy + j) * 2 + zl)

    @pl.loop(0, 8)
    def _(b):
        cells = gp[:, pl.ds(2 * b, 4)].reshape(512, 256)
        term = jnp.dot(ta[...], cells, preferred_element_type=F32).reshape(2, 2, 3, 32, 256)
        rows = term[:, :, 1] + shifted(term[:, :, 0], -1) + shifted(term[:, :, 2], 1)
        out_v[:, pl.ds(2 * b, 2)] = rows.astype(BF)

    for x in range(2):
        turned = jnp.swapaxes(out_v[x].astype(F32), 0, 1)
        out_t[:, x] = turned.astype(BF)


    @pl.loop(1, NXY)
    def _(j):
        wait(ra1.at[0], qa1.at[xymod(xy + j)])

    sa[...] = jnp.sum(ra1[...].astype(F32), axis=0).astype(BF)

    @pl.loop(1, NXY)
    def _(j):
        t = xymod(me2 + j)
        send(sa, ra2.at[me2], sa2.at[j], qa2.at[me2], t // 2, xy * 2 + lax.rem(t, 2))

    ra2[me2] = sa[...]

    @pl.loop(1, NXY)
    def _(j):
        wait(ra2.at[0], qa2.at[xymod(me2 + j)])

    ra3[xy] = jnp.sum(ra2[...].astype(F32), axis=0).astype(BF)

    @pl.loop(1, NXY)
    def _(j):
        k = xymod(xy + j)
        send(ra3.at[xy], ra3.at[xy], sa3.at[j], qa3.at[xy], f, k * 2 + zl)

    for h in range(2):

        @pl.when(xy != 2 * f + h)
        def _():
            wait(fin.at[h], qb3.at[h])

    scale_b = 1.0 / math.sqrt(ns * NF * ROWS * 128)
    scale_a = 1.0 / math.sqrt(8 * ns * NF * ROWS * 128)

    def unfold(full, per, target, scale):
        for dx in range(3):
            for dy in range(3):
                r0 = ((2 - dx) * 3 + 2 - dy) * per
                for dz in range(3):
                    target[9 * dx + 3 * dy + dz] = (
                        full[r0 : r0 + per, dz * 32 : dz * 32 + 32] * scale
                    )

    unfold(fin[...].reshape(96, 128), 8, gwb_out, scale_b)

    @pl.loop(1, NXY)
    def _(j):
        wait(grid_b.at[0, 0], s1.at[j])
        wait(gwb.at[0], sb1.at[j])
        wait(gwa.at[0], sa1.at[j])
        wait(sa, sa2.at[j])

    @pl.loop(0, NXY)
    def _(j):
        wait(grid_b.at[0, 0], sf.at[j])

    @pl.loop(1, 4)
    def _(j):
        wait(wb0, sw.at[j])

    @pl.loop(0, 4)
    def _(j):
        wait(wb0, sx.at[j])

    wait(pool2.at[0], spool.at[0])
    for n, (src, dst, df, dp) in enumerate(pre_moves):
        wait(src, sp.at[n])
    for n, (src, dst, slot, tf, tp) in enumerate(coarse_moves):
        wait(src, sc.at[n])

    for zt in range(2):

        @pl.when((f != owner) | (zl != zt))
        def _():
            wait(sb, sb2.at[zt])

    @pl.when(f == owner)
    def _():
        @pl.loop(1, NXY)
        def _(j):
            wait(fin.at[0], sb3.at[j])


    @pl.loop(1, NXY)
    def _(j):
        wait(ra3.at[0], qa3.at[xymod(xy + j)])

    packed = ra3[...].astype(F32).reshape(256, 128)
    rest = None
    lane = lax.broadcasted_iota(jnp.int32, (72, 128), 1)
    for n in range(3):
        piece = pltpu.roll(packed[n * 72 : n * 72 + 72], 32 * (n + 1), 1)
        rest = piece if n == 0 else jnp.where(lane < 32 * n, rest, piece)
    full = jnp.concatenate([packed[:216], rest], axis=0)
    unfold(full, 32, gwa_out, scale_a)

    @pl.loop(1, NXY)
    def _(j):
        wait(ra3.at[0], sa3.at[j])


def per_device(activation, preact, grad_out, weight_a, weight_b):
    hbm = pl.BlockSpec(memory_space=pltpu.HBM)
    vmem = pl.BlockSpec(memory_space=pltpu.VMEM)
    dma = pltpu.SemaphoreType.DMA
    out, gwa, gwb = pl.pallas_call(
        kernel,
        out_shape=(
            jax.ShapeDtypeStruct((32, 2, 16, 256), BF),
            jax.ShapeDtypeStruct((27, 32, 32), F32),
            jax.ShapeDtypeStruct((27, 8, 32), F32),
        ),
        in_specs=[hbm] * 5,
        out_specs=(vmem,) * 3,
        scratch_shapes=[
            pltpu.VMEM((8, 64, 128), BF),
            pltpu.VMEM((32, 2, 16, 256), BF),
            pltpu.VMEM((32, 2, 16, 256), BF),
            pltpu.VMEM((27, 32, 32), BF),
            pltpu.VMEM((27, 8, 32), BF),
            pltpu.VMEM((528, 128), BF),
            pltpu.VMEM((96, 128), BF),
            pltpu.VMEM((NF, 4, 48, 128), BF),
            pltpu.VMEM((NF, 96, 128), BF),
            pltpu.VMEM((384, 1024), BF),
            pltpu.VMEM((384, 512), BF),
            pltpu.VMEM((4, 18, 32, 256), BF),
            pltpu.VMEM((ROWS, 32, 128), BF),
            pltpu.VMEM((2, 4, 32, 128), BF),
            pltpu.VMEM((512, 256), BF),
            pltpu.VMEM((2, 4, 32, 128), BF),
            pltpu.VMEM((3, 10, 32, 128), BF),
            pltpu.VMEM((4, 18, 32, 256), BF),
            pltpu.VMEM((2, 16, 32, 256), F32),
            pltpu.VMEM((8, 512, 256), BF),
            pltpu.VMEM((512, 512), F32),
            pltpu.VMEM((2, 16, 32, 256), BF),
            pltpu.VMEM((NXY, 48, 128), BF),
            pltpu.VMEM((NXY, 48, 128), BF),
            pltpu.VMEM((NXY, 48, 128), BF),
            pltpu.VMEM((48, 128), BF),
            pltpu.VMEM((2, 48, 128), F32),
            pltpu.VMEM((NXY, 16, 128), BF),
            pltpu.VMEM((NXY, 16, 128), BF),
            pltpu.VMEM((NXY, 16, 128), BF),
            pltpu.VMEM((NXY, 16, 128), BF),
            pltpu.VMEM((16, 128), BF),
            dma((5,)),
            dma((NXY,)),
            dma((NXY,)),
            dma((NXY,)),
            dma((NXY,)),
            dma((NF,)),
            dma((NF,)),
            dma((4,)),
            dma((1,)),
            dma((1,)),
            dma((8,)),
            dma((8,)),
            dma((7,)),
            dma((7,)),
            dma((NXY,)),
            dma((NXY,)),
            dma((2,)),
            dma((NXY,)),
            dma((NXY,)),
            dma((2,)),
            dma((NXY,)),
            dma((NXY,)),
            dma((NXY,)),
            dma((NXY,)),
            dma((NXY,)),
            dma((NXY,)),
        ],
        compiler_params=pltpu.CompilerParams(
            collective_id=0, has_side_effects=True, vmem_limit_bytes=32 * 1024 * 1024
        ),
    )(
        *(
            pltpu.with_memory_space_constraint(x, pltpu.HBM)
            for x in (grad_out.reshape(8, 64, 128), preact, activation, weight_a, weight_b)
        )
    )
    return (out, gwa, gwb)


def solution(mesh):
    placed = (
        P(None, "space", "filt", None),
        P(None, "space", "filt", None),
        P("filt", "space", None, None),
        P(),
        P(None, "filt", None),
    )
    return jax.shard_map(
        per_device,
        mesh=mesh,
        in_specs=placed,
        out_specs=(P(None, "space", "filt", None), P(), P(None, "filt", None)),
        check_vma=False,
    )
```

time: 77.2 us -> 60.8 us (0.79)
  Pallas kernels: 67.5 us -> 57.8 us
  local copies, waits for them, and re-layouts: 8.52 us -> 2.2 us
    pallas_call x1, Pallas kernels: 67.5 us -> 57.8 us  [per_device(): pl.pallas_call(kernel, out_shape=(jax.ShapeDtypeStruct((32, 2, 16, 256),...]
    transpose x6 -> x0, local copies, waits for them, and re-layouts: 2.21 us -> none  [the longest x2 0.92 us: per_device(): grad_wa = jnp.transpose(full, (0, 1, 3, 2, 4)).reshape(27, 32, 32)]
    unnamed x12 -> x3, local copies, waits for them, and re-layouts: 4.03 us -> 2.2 us
    reshape x10 -> x0, local copies, waits for them, and re-layouts: 1.26 us -> none  [the longest x3 0.52 us: tap_rows(): return parts.reshape(3 * i, 16 * o)]
where the time goes in v2:
time: 60.8 us; the launch traced here: 60.7 us
  Pallas kernels  57.8 us (95%)
  local copies, waits for them, and re-layouts  2.2 us (4%)
  between operations  0.64 us (1%)
    pallas_call x1, Pallas kernels, per_device(): pl.pallas_call(kernel, out_shape=(jax.ShapeDtypeStruct((32, 2, 16, 256),...  57.8 us
    unnamed x3, local copies, waits for them, and re-layouts  2.2 us

profile of v2, /device:TPU:1, one launch (start us, length us, event | category | flops | bytes accessed | tf_op | source)
XLA Modules:
  0.0 60.7 jit_solution(12860767457243271063)
XLA Ops:
  0.6 57.8 %shard_map.76 = (bf16[32,2,16,256]{3,2,1,0:T(8,128)(2,1)S(1)}, f32[27,32,32]{2,1,0:T(8,128)S(1)}, f32[27,8,32]{2,1,0:T(8,128)S(1)}) custom-call(bf16[8,64,128]{2,1,0:T(8,128)(2,1)} %bitcast.1, bf16[32,2,16,256]{3,2,1,0:T(8,128)(2,1)} %pre_h.1, bf16[32,2,16,256]{3,2,1,0:T(8,128)(2,1)} %act_h.1, bf16[27,32,32]{2,1,0:T(8,128)(2,1)} %wa_h.1, bf16[27,8,32]{2,1,0:T(8,128)(2,1)} %wb_h.1), custom_call_target="tpu_custom_call" | custom-call | tf_op jit(solution)/shard_map/pallas_call | solution.py:623
  58.5 0.8 %copy.11 = bf16[32,2,16,256]{3,2,1,0:T(8,128)(2,1)} copy(bf16[32,2,16,256]{3,2,1,0:T(8,128)(2,1)S(1)} %get-tuple-element.6) | data formatting | bytes 1048576
  59.3 0.8 %copy.12 = f32[27,32,32]{2,1,0:T(8,128)} copy(f32[27,32,32]{2,1,0:T(8,128)S(1)} %get-tuple-element.7) | data formatting | bytes 221184
  60.0 0.6 %copy.13 = f32[27,8,32]{2,1,0:T(8,128)} copy(f32[27,8,32]{2,1,0:T(8,128)S(1)} %get-tuple-element.8) | data formatting | bytes 55296

commit v3 on v2

--- a/solution.py
+++ b/solution.py
@@ -12,7 +12,10 @@
 NF = 8
 ROWS = 8
 NXY = 16
-PRE_AT = 5
+
+
+FAR_XY = (10, 9, 11, 6, 14, 8, 2, 5, 7, 13, 15, 1, 3, 4, 12)
+FAR_Z = (8, 7, 9, 6, 10, 5, 11, 4, 12, 3, 13, 14, 15, 1, 2)
 
 
 def shifted(values, step):
@@ -131,21 +134,21 @@
             device_id_type=pl.DeviceIdType.MESH,
         )
 
-    @pl.loop(1, NXY)
-    def _(j):
-        t = xymod(me2 + j)
-        greet(t // 2, xy * 2 + lax.rem(t, 2))
-
-    @pl.loop(1, NXY)
-    def _(j):
-        greet(f, xymod(xy + j) * 2 + zl)
-
     cross = xymod(xy + 2 * zl - 1) * 2 + 1 - zl
     greet(f, cross)
     greet(fmod(f - 1), cross)
     greet(fmod(f + 1), cross)
     greet(fmod(f - 1), xymod(xy + 1) * 2 + zl)
     greet(fmod(f + 1), xymod(xy - 1) * 2 + zl)
+
+    @pl.loop(1, NXY)
+    def _(j):
+        t = xymod(me2 + j)
+        greet(t // 2, xy * 2 + lax.rem(t, 2))
+
+    @pl.loop(1, NXY)
+    def _(j):
+        greet(f, xymod(xy + j) * 2 + zl)
 
     loads = [
         pltpu.make_async_copy(src, dst, sin.at[n])
@@ -229,14 +232,6 @@
         (prh.at[2, 1], prh.at[0, 17], -1, 1),
         (prh.at[2, 16], prh.at[0, 0], 1, 1),
     )
-
-    def send_pre(first=0, last=8):
-        for n in range(first, last):
-            src, dst, df, dp = pre_moves[n]
-            send(src, dst, sp.at[n], rp.at[n], fmod(f + df), smod(p + dp))
-
-    if PRE_AT == 0:
-        send_pre()
 
     grid_b[f, 1 + zl] = gsrc[pl.ds(pl.multiple_of(me2 * 32, 16), 48)]
 
@@ -274,28 +269,21 @@
     )
     pool2[zl] = pool[pl.ds(4 * zl, 4)]
 
-    if PRE_AT == 7:
-        send_pre(0, 1)
     @pl.loop(1, 4)
     def _(j):
         s = fmod(f - 2 * j)
         wait(wb0, rw.at[s])
         send(wb_all.at[s], wb_all.at[s], sx.at[j], rw.at[s], sibling, p)
 
-    if PRE_AT == 5:
-        send_pre()
-    if PRE_AT == 6:
-        send_pre(0, 1)
+    for n, (src, dst, df, dp) in enumerate(pre_moves):
+        send(src, dst, sp.at[n], rp.at[n], fmod(f + df), smod(p + dp))
+
     @pl.loop(1, NXY)
     def _(j):
         s = xymod(me2 - j)
         wait(grid_b.at[0, 0], r1.at[s])
         forward(s)
 
-    if PRE_AT == 1:
-        send_pre()
-    if PRE_AT in (6, 7):
-        send_pre(1, 8)
 
     loads[3].wait()
     wide_a = arranged(waraw, 32, 128, 32)
@@ -389,16 +377,15 @@
     for x in range(2):
         actt[x] = jnp.swapaxes(araw[:, x].astype(F32), 0, 1)
 
-    @pl.loop(0, 8)
-    def _(b):
+    for b in range(8):
         for x2 in range(2):
             for y2 in range(2):
                 wide = actt[x2, 2 * b + y2]
-                base = (x2 * 2 + y2) * 128
-                act3[b, base : base + 32] = shifted(wide, 1).astype(BF)
-                act3[b, base + 32 : base + 64] = wide.astype(BF)
-                act3[b, base + 64 : base + 96] = shifted(wide, -1).astype(BF)
-                act3[b, base + 96 : base + 128] = jnp.zeros((32, 256), BF)
+                r0, c0 = (x2 * 2 + y2) * 128, b * 256
+                act3[r0 : r0 + 32, c0 : c0 + 256] = shifted(wide, 1).astype(BF)
+                act3[r0 + 32 : r0 + 64, c0 : c0 + 256] = wide.astype(BF)
+                act3[r0 + 64 : r0 + 96, c0 : c0 + 256] = shifted(wide, -1).astype(BF)
+                act3[r0 + 96 : r0 + 128, c0 : c0 + 256] = jnp.zeros((32, 256), BF)
 
     @pl.loop(1, NXY)
     def _(j):
@@ -453,13 +440,16 @@
                             prh[xh, yh] > jnp.zeros((), BF), fine[row], jnp.zeros((), BF)
                         )
 
-    racc[...] = jnp.zeros(racc.shape, F32)
-
-    @pl.loop(0, 8)
-    def _(b):
-        cells = gp[:, pl.ds(2 * b, 4)].reshape(512, 256)
-        racc[...] += lax.dot_general(
-            cells, act3[b], (((1,), (1,)), ((), ())), preferred_element_type=F32
+    cells = jnp.concatenate(
+        [gp[:, 2 * b : 2 * b + 4].reshape(512, 256) for b in range(8)], axis=1
+    )
+    for x2 in range(2):
+        r0, c0 = 128 * x2, 256 * x2
+        racc[r0 : r0 + 384, c0 : c0 + 256] = lax.dot_general(
+            cells[r0 : r0 + 384],
+            act3[c0 : c0 + 256],
+            (((1,), (1,)), ((), ())),
+            preferred_element_type=F32,
         )
 
     taps = []
@@ -481,8 +471,7 @@
     packed = jnp.concatenate([packed, jnp.zeros((40, 128), F32)], axis=0)
     gwa[...] = packed.astype(BF).reshape(NXY, 16, 128)
 
-    @pl.loop(1, NXY)
-    def _(j):
+    for j in FAR_XY:
         k = xymod(xy + j)
         send(gwa.at[k], ra1.at[xy], sa1.at[j], qa1.at[xy], f, k * 2 + zl)
 
@@ -504,12 +493,11 @@
         def _(j):
             send(fin.at[half], fin.at[half], sb3.at[j], qb3.at[half], f, xymod(xy + j) * 2 + zl)
 
-    @pl.loop(0, 8)
-    def _(b):
-        cells = gp[:, pl.ds(2 * b, 4)].reshape(512, 256)
+    for b in range(8):
+        cells = gp[:, 2 * b : 2 * b + 4].reshape(512, 256)
         term = jnp.dot(ta[...], cells, preferred_element_type=F32).reshape(2, 2, 3, 32, 256)
         rows = term[:, :, 1] + shifted(term[:, :, 0], -1) + shifted(term[:, :, 2], 1)
-        out_v[:, pl.ds(2 * b, 2)] = rows.astype(BF)
+        out_v[:, 2 * b : 2 * b + 2] = rows.astype(BF)
 
     for x in range(2):
         turned = jnp.swapaxes(out_v[x].astype(F32), 0, 1)
@@ -522,8 +510,7 @@
 
     sa[...] = jnp.sum(ra1[...].astype(F32), axis=0).astype(BF)
 
-    @pl.loop(1, NXY)
-    def _(j):
+    for j in FAR_Z:
         t = xymod(me2 + j)
         send(sa, ra2.at[me2], sa2.at[j], qa2.at[me2], t // 2, xy * 2 + lax.rem(t, 2))
 
@@ -535,8 +522,7 @@
 
     ra3[xy] = jnp.sum(ra2[...].astype(F32), axis=0).astype(BF)
 
-    @pl.loop(1, NXY)
-    def _(j):
+    for j in FAR_XY:
         k = xymod(xy + j)
         send(ra3.at[xy], ra3.at[xy], sa3.at[j], qa3.at[xy], f, k * 2 + zl)
 
@@ -649,7 +635,7 @@
             pltpu.VMEM((3, 10, 32, 128), BF),
             pltpu.VMEM((4, 18, 32, 256), BF),
             pltpu.VMEM((2, 16, 32, 256), F32),
-            pltpu.VMEM((8, 512, 256), BF),
+            pltpu.VMEM((512, 2048), BF),
             pltpu.VMEM((512, 512), F32),
             pltpu.VMEM((2, 16, 32, 256), BF),
             pltpu.VMEM((NXY, 48, 128), BF),

time: 60.8 us -> 57.8 us (0.951)
  Pallas kernels: 57.8 us -> 54.9 us
    pallas_call x1, Pallas kernels: 57.8 us -> 54.9 us  [per_device(): pl.pallas_call(kernel, out_shape=(jax.ShapeDtypeStruct((32, 2, 16, 256),...]
where the time goes in v3:
time: 57.8 us; the launch traced here: 57.7 us
  Pallas kernels  54.9 us (95%)
  local copies, waits for them, and re-layouts  2.2 us (4%)
  between operations  0.64 us (1%)
    pallas_call x1, Pallas kernels, per_device(): pl.pallas_call(kernel, out_shape=(jax.ShapeDtypeStruct((32, 2, 16, 256),...  54.9 us
    unnamed x3, local copies, waits for them, and re-layouts  2.2 us

profile of v3, /device:TPU:1, one launch (start us, length us, event | category | flops | bytes accessed | tf_op | source)
XLA Modules:
  0.0 57.7 jit_solution(11932274109980753832)
XLA Ops:
  0.6 54.9 %shard_map.76 = (bf16[32,2,16,256]{3,2,1,0:T(8,128)(2,1)S(1)}, f32[27,32,32]{2,1,0:T(8,128)S(1)}, f32[27,8,32]{2,1,0:T(8,128)S(1)}) custom-call(bf16[8,64,128]{2,1,0:T(8,128)(2,1)} %bitcast.1, bf16[32,2,16,256]{3,2,1,0:T(8,128)(2,1)} %pre_h.1, bf16[32,2,16,256]{3,2,1,0:T(8,128)(2,1)} %act_h.1, bf16[27,32,32]{2,1,0:T(8,128)(2,1)} %wa_h.1, bf16[27,8,32]{2,1,0:T(8,128)(2,1)} %wb_h.1), custom_call_target="tpu_custom_call" | custom-call | tf_op jit(solution)/shard_map/pallas_call | solution.py:609
  55.5 0.8 %copy.11 = bf16[32,2,16,256]{3,2,1,0:T(8,128)(2,1)} copy(bf16[32,2,16,256]{3,2,1,0:T(8,128)(2,1)S(1)} %get-tuple-element.6) | data formatting | bytes 1048576
  56.3 0.8 %copy.12 = f32[27,32,32]{2,1,0:T(8,128)} copy(f32[27,32,32]{2,1,0:T(8,128)S(1)} %get-tuple-element.7) | data formatting | bytes 221184
  57.1 0.6 %copy.13 = f32[27,8,32]{2,1,0:T(8,128)} copy(f32[27,8,32]{2,1,0:T(8,128)S(1)} %get-tuple-element.8) | data formatting | bytes 55296

commit v4 on v3

--- a/solution.py
+++ b/solution.py
@@ -195,9 +195,10 @@
     core = lax.rem(f, 2)
     sibling = f + 1 - 2 * core
 
-    @pl.loop(1, 4)
-    def _(j):
-        send(wb0, wb_all.at[f], sw.at[j], rw.at[f], fmod(f + 2 * j), p)
+    toward = fmod(f + 4 * zl - 2)
+    send(wb0, wb_all.at[f], sw.at[1], rw.at[f], fmod(f + 4), xy * 2 + 1 - zl)
+    send(wb0, wb_all.at[f], sw.at[2], rw.at[f], toward, p)
+    send(wb0, wb_all.at[f], sw.at[3], rw.at[f], toward, xy * 2 + 1 - zl)
 
     send(wb0, wb_all.at[f], sx.at[0], rw.at[f], sibling, p)
     wb_all[f] = wb0[...]
@@ -269,14 +270,13 @@
     )
     pool2[zl] = pool[pl.ds(4 * zl, 4)]
 
-    @pl.loop(1, 4)
-    def _(j):
+    for n, (src, dst, df, dp) in enumerate(pre_moves):
+        send(src, dst, sp.at[n], rp.at[n], fmod(f + df), smod(p + dp))
+
+    for j in (1, 3, 2):
         s = fmod(f - 2 * j)
         wait(wb0, rw.at[s])
         send(wb_all.at[s], wb_all.at[s], sx.at[j], rw.at[s], sibling, p)
-
-    for n, (src, dst, df, dp) in enumerate(pre_moves):
-        send(src, dst, sp.at[n], rp.at[n], fmod(f + df), smod(p + dp))
 
     @pl.loop(1, NXY)
     def _(j):

time: 57.8 us -> 57.1 us (0.988)
  Pallas kernels: 54.9 us -> 54.1 us
    pallas_call x1, Pallas kernels: 54.9 us -> 54.1 us  [per_device(): pl.pallas_call(kernel, out_shape=(jax.ShapeDtypeStruct((32, 2, 16, 256),...]
where the time goes in v4:
time: 57.1 us; the launch traced here: 57 us
  Pallas kernels  54.1 us (95%)
  local copies, waits for them, and re-layouts  2.2 us (4%)
  between operations  0.64 us (1%)
    pallas_call x1, Pallas kernels, per_device(): pl.pallas_call(kernel, out_shape=(jax.ShapeDtypeStruct((32, 2, 16, 256),...  54.1 us
    unnamed x3, local copies, waits for them, and re-layouts  2.2 us

profile of v4, /device:TPU:1, one launch (start us, length us, event | category | flops | bytes accessed | tf_op | source)
XLA Modules:
  0.0 57.0 jit_solution(11344329665318172927)
XLA Ops:
  0.6 54.1 %shard_map.76 = (bf16[32,2,16,256]{3,2,1,0:T(8,128)(2,1)S(1)}, f32[27,32,32]{2,1,0:T(8,128)S(1)}, f32[27,8,32]{2,1,0:T(8,128)S(1)}) custom-call(bf16[8,64,128]{2,1,0:T(8,128)(2,1)} %bitcast.1, bf16[32,2,16,256]{3,2,1,0:T(8,128)(2,1)} %pre_h.1, bf16[32,2,16,256]{3,2,1,0:T(8,128)(2,1)} %act_h.1, bf16[27,32,32]{2,1,0:T(8,128)(2,1)} %wa_h.1, bf16[27,8,32]{2,1,0:T(8,128)(2,1)} %wb_h.1), custom_call_target="tpu_custom_call" | custom-call | tf_op jit(solution)/shard_map/pallas_call | solution.py:609
  54.8 0.8 %copy.11 = bf16[32,2,16,256]{3,2,1,0:T(8,128)(2,1)} copy(bf16[32,2,16,256]{3,2,1,0:T(8,128)(2,1)S(1)} %get-tuple-element.6) | data formatting | bytes 1048576
  55.6 0.8 %copy.12 = f32[27,32,32]{2,1,0:T(8,128)} copy(f32[27,32,32]{2,1,0:T(8,128)S(1)} %get-tuple-element.7) | data formatting | bytes 221184
  56.3 0.6 %copy.13 = f32[27,8,32]{2,1,0:T(8,128)} copy(f32[27,8,32]{2,1,0:T(8,128)S(1)} %get-tuple-element.8) | data formatting | bytes 55296

commit v5 on v4

--- a/solution.py
+++ b/solution.py
@@ -387,18 +387,6 @@
                 act3[r0 + 64 : r0 + 96, c0 : c0 + 256] = shifted(wide, -1).astype(BF)
                 act3[r0 + 96 : r0 + 128, c0 : c0 + 256] = jnp.zeros((32, 256), BF)
 
-    @pl.loop(1, NXY)
-    def _(j):
-        wait(rb1.at[0], qb1.at[xymod(xy + j)])
-
-    owner = xy // 2
-    sb[...] = jnp.sum(rb1[...].astype(F32), axis=0).astype(BF)
-    for zt in range(2):
-
-        @pl.when((f != owner) | (zl != zt))
-        def _():
-            send(sb, rb2.at[me2], sb2.at[zt], qb2.at[me2], owner, xy * 2 + zt)
-
     wait(gpo, rc.at[0])
     for n in range(2):
         wait(gpo.at[0], rc.at[1 + n])
@@ -477,21 +465,17 @@
 
     ra1[xy] = gwa[xy]
 
-    half = lax.rem(xy, 2)
-
-    @pl.when(f == owner)
-    def _():
-        rb2[me2] = sb[...]
-
-        @pl.loop(1, NXY)
-        def _(j):
-            wait(rb2.at[0], qb2.at[xymod(me2 + j)])
-
-        fin[half] = jnp.sum(rb2[...].astype(F32), axis=0)
-
-        @pl.loop(1, NXY)
-        def _(j):
-            send(fin.at[half], fin.at[half], sb3.at[j], qb3.at[half], f, xymod(xy + j) * 2 + zl)
+    @pl.loop(1, NXY)
+    def _(j):
+        wait(rb1.at[0], qb1.at[xymod(xy + j)])
+
+    owner = xy // 2
+    sb[...] = jnp.sum(rb1[...].astype(F32), axis=0).astype(BF)
+    for zt in range(2):
+
+        @pl.when((f != owner) | (zl != zt))
+        def _():
+            send(sb, rb2.at[me2], sb2.at[zt], qb2.at[me2], owner, xy * 2 + zt)
 
     for b in range(8):
         cells = gp[:, 2 * b : 2 * b + 4].reshape(512, 256)
@@ -515,6 +499,22 @@
         send(sa, ra2.at[me2], sa2.at[j], qa2.at[me2], t // 2, xy * 2 + lax.rem(t, 2))
 
     ra2[me2] = sa[...]
+
+    half = lax.rem(xy, 2)
+
+    @pl.when(f == owner)
+    def _():
+        rb2[me2] = sb[...]
+
+        @pl.loop(1, NXY)
+        def _(j):
+            wait(rb2.at[0], qb2.at[xymod(me2 + j)])
+
+        fin[half] = jnp.sum(rb2[...].astype(F32), axis=0)
+
+        @pl.loop(1, NXY)
+        def _(j):
+            send(fin.at[half], fin.at[half], sb3.at[j], qb3.at[half], f, xymod(xy + j) * 2 + zl)
 
     @pl.loop(1, NXY)
     def _(j):

time: 57.1 us -> 56.7 us (level)
  no operation moved by 1% of the time
where the time goes in v5:
time: 56.7 us; the launch traced here: 56.6 us
  Pallas kernels  53.8 us (95%)
  local copies, waits for them, and re-layouts  2.2 us (4%)
  between operations  0.64 us (1%)
    pallas_call x1, Pallas kernels, per_device(): pl.pallas_call(kernel, out_shape=(jax.ShapeDtypeStruct((32, 2, 16, 256),...  53.8 us
    unnamed x3, local copies, waits for them, and re-layouts  2.2 us

profile of v5, /device:TPU:1, one launch (start us, length us, event | category | flops | bytes accessed | tf_op | source)
XLA Modules:
  0.0 56.6 jit_solution(724886640111745652)
XLA Ops:
  0.6 53.8 %shard_map.76 = (bf16[32,2,16,256]{3,2,1,0:T(8,128)(2,1)S(1)}, f32[27,32,32]{2,1,0:T(8,128)S(1)}, f32[27,8,32]{2,1,0:T(8,128)S(1)}) custom-call(bf16[8,64,128]{2,1,0:T(8,128)(2,1)} %bitcast.1, bf16[32,2,16,256]{3,2,1,0:T(8,128)(2,1)} %pre_h.1, bf16[32,2,16,256]{3,2,1,0:T(8,128)(2,1)} %act_h.1, bf16[27,32,32]{2,1,0:T(8,128)(2,1)} %wa_h.1, bf16[27,8,32]{2,1,0:T(8,128)(2,1)} %wb_h.1), custom_call_target="tpu_custom_call" | custom-call | tf_op jit(solution)/shard_map/pallas_call | solution.py:609
  54.4 0.8 %copy.11 = bf16[32,2,16,256]{3,2,1,0:T(8,128)(2,1)} copy(bf16[32,2,16,256]{3,2,1,0:T(8,128)(2,1)S(1)} %get-tuple-element.6) | data formatting | bytes 1048576
  55.2 0.8 %copy.12 = f32[27,32,32]{2,1,0:T(8,128)} copy(f32[27,32,32]{2,1,0:T(8,128)S(1)} %get-tuple-element.7) | data formatting | bytes 221184
  56.0 0.6 %copy.13 = f32[27,8,32]{2,1,0:T(8,128)} copy(f32[27,8,32]{2,1,0:T(8,128)S(1)} %get-tuple-element.8) | data formatting | bytes 55296

commit v6 on v5

--- a/solution.py
+++ b/solution.py
@@ -285,13 +285,6 @@
         forward(s)
 
 
-    loads[3].wait()
-    wide_a = arranged(waraw, 32, 128, 32)
-    for n, turn in enumerate((0, 32, 128, 160)):
-        ta[n * 96 : n * 96 + 96] = (
-            pltpu.roll(wide_a, turn, 1) if turn else wide_a
-        ).astype(BF)
-
     @pl.loop(0, 4)
     def _(j):
         wait(wb0, rw.at[2 * j + 1 - core])
@@ -476,6 +469,13 @@
         @pl.when((f != owner) | (zl != zt))
         def _():
             send(sb, rb2.at[me2], sb2.at[zt], qb2.at[me2], owner, xy * 2 + zt)
+
+    loads[3].wait()
+    wide_a = arranged(waraw, 32, 128, 32)
+    for n, turn in enumerate((0, 32, 128, 160)):
+        ta[n * 96 : n * 96 + 96] = (
+            pltpu.roll(wide_a, turn, 1) if turn else wide_a
+        ).astype(BF)
 
     for b in range(8):
         cells = gp[:, 2 * b : 2 * b + 4].reshape(512, 256)

time: 56.7 us -> 56.7 us (level)
  no operation moved by 1% of the time
where the time goes in v6:
time: 56.7 us; the launch traced here: 56.6 us
  Pallas kernels  53.7 us (95%)
  local copies, waits for them, and re-layouts  2.2 us (4%)
  between operations  0.64 us (1%)
    pallas_call x1, Pallas kernels, per_device(): pl.pallas_call(kernel, out_shape=(jax.ShapeDtypeStruct((32, 2, 16, 256),...  53.7 us
    unnamed x3, local copies, waits for them, and re-layouts  2.2 us

profile of v6, /device:TPU:1, one launch (start us, length us, event | category | flops | bytes accessed | tf_op | source)
XLA Modules:
  0.0 56.6 jit_solution(5906173736690827402)
XLA Ops:
  0.6 53.7 %shard_map.76 = (bf16[32,2,16,256]{3,2,1,0:T(8,128)(2,1)S(1)}, f32[27,32,32]{2,1,0:T(8,128)S(1)}, f32[27,8,32]{2,1,0:T(8,128)S(1)}) custom-call(bf16[8,64,128]{2,1,0:T(8,128)(2,1)} %bitcast.1, bf16[32,2,16,256]{3,2,1,0:T(8,128)(2,1)} %pre_h.1, bf16[32,2,16,256]{3,2,1,0:T(8,128)(2,1)} %act_h.1, bf16[27,32,32]{2,1,0:T(8,128)(2,1)} %wa_h.1, bf16[27,8,32]{2,1,0:T(8,128)(2,1)} %wb_h.1), custom_call_target="tpu_custom_call" | custom-call | tf_op jit(solution)/shard_map/pallas_call | solution.py:609
  54.4 0.8 %copy.11 = bf16[32,2,16,256]{3,2,1,0:T(8,128)(2,1)} copy(bf16[32,2,16,256]{3,2,1,0:T(8,128)(2,1)S(1)} %get-tuple-element.6) | data formatting | bytes 1048576
  55.2 0.8 %copy.12 = f32[27,32,32]{2,1,0:T(8,128)} copy(f32[27,32,32]{2,1,0:T(8,128)S(1)} %get-tuple-element.7) | data formatting | bytes 221184
  55.9 0.6 %copy.13 = f32[27,8,32]{2,1,0:T(8,128)} copy(f32[27,8,32]{2,1,0:T(8,128)S(1)} %get-tuple-element.8) | data formatting | bytes 55296
